TPU v7x, 256 devices: a whole 4x4x8 slice. The times are simulated.
256 devices in a mesh: group: 2 (over core), dp: 16 (over y, x), mp: 8 (over z).
Axes of the slice: x: 4, y: 4, z: 8, core: 2. Of those that a mesh axis runs over, the one named last changes fastest.
Arguments:
- queries: bfloat16 [8192, 1024], P(('group', 'dp')), may hold values from -6 to 6
- clips: bfloat16 [65536, 1024], P(('group', 'dp')), may hold values from -6 to 6
- norm_gain: float32 [1024], replicated, may hold values from 0.1 to 1.9
- w_in: bfloat16 [1024, 2, 4096], P(None, None, 'mp'), may hold values from -0.1875 to 0.1875
- w_out: bfloat16 [4096, 1024], P('mp'), may hold values from -0.09375 to 0.09375
- proj: bfloat16 [1024, 768], replicated, may hold values from -0.1875 to 0.1875
- pos_row: int32 [8192], P(('group', 'dp', 'mp')), may hold values from 0 to 255
- neg_owner: int32 [8192, 8], P(('group', 'dp', 'mp')), may hold values from 0 to 127, all different within a row; in each aligned block of 32 rows (0 to 31, 32 to 63, ...) at most 8 rows name the same one
- neg_row: int32 [8192, 8], P(('group', 'dp', 'mp')), may hold values from 0 to 255
- clip_dest: int32 [65536, 1], P(('group', 'dp', 'mp')), may hold values from 0 to 31; in each aligned block of 256 rows (0 to 255, 256 to 511, ...) at most 16 rows name the same one
Outputs:
- losses: float32 [8192], P(('group', 'dp', 'mp'))
- index_shard: bfloat16 [131072, 768], P(('group', 'dp', 'mp'))
- grad_proj: float32 [1024, 768], P(('group', 'dp', 'mp'))
Inputs may be any that keep to these rules, and one draw needn't show every extreme that they name: `neg_owner`: each query's 8 owners differ. In each aligned block of 32 rows (the rows of one device) at most 8 rows name one owner, and some block reaches 8. `clip_dest`: in each aligned block of 256 rows (the clips of one device) at most 16 name one owner, and some block reaches 16.
All inputs are finite; a program needn't handle non-finite values.
Results may differ from a plain program's by a relative error of at most 0.013.
Values may be sent and summed in bfloat16 or wider, within the bound.
A program may use at most 128 MiB of HBM per device.

v0:
```python
import jax
import jax.numpy as jnp
from jax import lax
from jax.sharding import PartitionSpec as P

norm_eps = 1e-06
embed_eps = 1e-06
score_scale = 20.0


def slots_of(owner_ids, owners):
    onehot = (owner_ids[:, None] == jnp.arange(owners, dtype=jnp.int32)[None, :]).astype(jnp.int32)
    return jnp.sum(jnp.cumsum(onehot, axis=0) * onehot, axis=-1) - 1


def per_device(
    queries, clips, norm_gain, w_in, w_out, proj, pos_row, neg_owner, neg_row, clip_dest
):
    slices = lax.axis_size("mp")
    query_total, width = queries.shape
    query_rows = query_total // slices
    clip_rows = clips.shape[0] // slices
    per_block = query_rows + clip_rows
    hidden_local = w_out.shape[0]
    stacked = jnp.concatenate(
        [queries.reshape(slices, query_rows, width), clips.reshape(slices, clip_rows, width)],
        axis=1,
    ).reshape(slices * per_block, width)
    values = stacked.astype(jnp.float32)
    scale = lax.rsqrt(jnp.mean(values * values, axis=-1, keepdims=True) + norm_eps)
    normed = (values * scale * norm_gain).astype(jnp.bfloat16)
    start_row = lax.axis_index("mp") * per_block
    merged = w_in.reshape(width, 2 * hidden_local)
    both = jnp.dot(normed, merged, preferred_element_type=jnp.float32)
    hidden = (jax.nn.silu(both[:, :hidden_local]) * both[:, hidden_local:]).astype(jnp.bfloat16)
    mixed = lax.psum_scatter(
        jnp.dot(hidden, w_out, preferred_element_type=jnp.float32),
        "mp",
        scatter_dimension=0,
        tiled=True,
    )
    residual = lax.dynamic_slice_in_dim(values, start_row, per_block, 0)
    summed = (residual + mixed).astype(jnp.bfloat16)
    raw = jnp.dot(summed, proj, preferred_element_type=jnp.float32)
    length = jnp.sqrt(jnp.sum(raw * raw, axis=-1, keepdims=True) + embed_eps)
    unit = raw / length
    embedded = unit.astype(jnp.bfloat16)
    embed_width = embedded.shape[1]
    query_embed = embedded[:query_rows]
    clip_embed = embedded[query_rows:]
    query_unit = unit[:query_rows]
    query_length = length[:query_rows]
    query_summed = summed[:query_rows]
    owners = lax.axis_size(("group", "dp"))
    destination = clip_dest[:, 0]
    cap_index = max(2, min(clip_rows, 2 * clip_rows // owners))
    place_index = destination * cap_index + slots_of(destination, owners)
    outgoing = (
        jnp.zeros((owners * cap_index, embed_width), jnp.bfloat16).at[place_index].set(clip_embed)
    )
    received = lax.all_to_all(
        outgoing.reshape(owners, cap_index, embed_width),
        ("group", "dp"),
        split_axis=0,
        concat_axis=0,
        tiled=True,
    )
    index_shard = received.reshape(owners * cap_index, embed_width)
    peers = lax.axis_size(("dp", "mp"))
    negatives = neg_owner.shape[1]
    cap_fetch = max(2, min(query_rows, 4 * query_rows * negatives // peers))
    flat_owner = neg_owner.reshape(-1)
    place_fetch = flat_owner * cap_fetch + slots_of(flat_owner, peers)
    wanted = jnp.zeros((peers * cap_fetch,), jnp.int32).at[place_fetch].set(neg_row.reshape(-1))
    fetched = lax.all_to_all(
        clip_embed[
            lax.all_to_all(
                wanted.reshape(peers, cap_fetch),
                ("dp", "mp"),
                split_axis=0,
                concat_axis=0,
                tiled=True,
            )
        ],
        ("dp", "mp"),
        split_axis=0,
        concat_axis=0,
        tiled=True,
    )
    negative_embed = fetched.reshape(peers * cap_fetch, embed_width)[place_fetch].reshape(
        query_rows, negatives, embed_width
    )
    positive_embed = clip_embed[pos_row]
    candidates = jnp.concatenate([positive_embed[:, None, :], negative_embed], axis=1).astype(
        jnp.float32
    )
    scores = score_scale * jnp.einsum("qe,qce->qc", query_embed.astype(jnp.float32), candidates)
    weights = jnp.exp(scores)
    total = jnp.sum(weights, axis=-1)
    losses = jnp.log(total) - scores[:, 0]
    probs = weights / total[:, None]
    dunit = score_scale * (jnp.einsum("qc,qce->qe", probs, candidates) - candidates[:, 0, :])
    along = jnp.sum(query_unit * dunit, axis=-1, keepdims=True)
    draw = ((dunit - query_unit * along) / query_length).astype(jnp.bfloat16)
    term = lax.dot_general(
        query_summed, draw, (((0,), (0,)), ((), ())), preferred_element_type=jnp.float32
    )
    grad_proj = lax.psum_scatter(term, ("group", "dp", "mp"), scatter_dimension=0, tiled=True)
    return (losses, index_shard, grad_proj)


def solution(mesh):
    return jax.shard_map(
        per_device,
        mesh=mesh,
        in_specs=(
            P(("group", "dp"), None),
            P(("group", "dp"), None),
            P(),
            P(None, None, "mp"),
            P("mp", None),
            P(),
            P(("group", "dp", "mp")),
            P(("group", "dp", "mp"), None),
            P(("group", "dp", "mp"), None),
            P(("group", "dp", "mp"), None),
        ),
        out_specs=(
            P(("group", "dp", "mp")),
            P(("group", "dp", "mp"), None),
            P(("group", "dp", "mp"), None),
        ),
        check_vma=False,
    )
```

profile of v0, /device:TPU:1, one launch (start us, length us, event | category | flops | bytes accessed | tf_op | source)
XLA Modules:
  0.0 475.7 jit_solution(2439881388576834608)
XLA Ops:
  7.2 0.0 copy-start
  7.2 0.0 copy-start.2
  7.2 0.0 reduce-scatter.2.cloned.1.call-start
  7.2 0.0 copy-start.1
  7.3 3.5 multiply_reduce_fusion
  10.7 2.2 copy.37
  12.9 1.3 multiply_convert_fusion
  14.2 0.0 copy-start.13
  14.2 5.1 %fusion.30 = f32[2304,1024]{1,0:T(8,128)S(1)} fusion(bf16[2304,1024]{1,0:T(8,128)(2,1)S(1)} %bitcast.86, bf16[1024,1024]{1,0:T(8,128)(2,1)S(1)} %bitcast.89), kind=kOutput, calls=%fused_computation.73 | convolution fusion | flops 4831838208 | bytes 16252928 | tf_op jit(solution)/shard_map/dot_general | solution.py:34
  19.3 5.1 %fusion.1 = f32[2304,1024]{1,0:T(8,128)} fusion(bf16[512,1024]{1,0:T(8,128)(2,1)S(1)} %copy-done.13, f32[2304,1024]{1,0:T(8,128)S(1)} %fusion.30), kind=kOutput, calls=%fused_computation.10 | convolution fusion | flops 2422996992 | bytes 19922944 | tf_op jit(solution)/shard_map/dot_general | solution.py:37
  24.4 0.0 reduce-scatter.2.cloned.1.call-update
  24.5 0.7 copy-done.8
  25.1 0.1 copy.24
  25.2 0.1 eq.54
  25.3 0.1 eq.50
  25.4 0.1 copy.26
  25.5 0.2 fusion.7
  25.8 0.1 copy.23
  25.9 0.1 mul.110
  26.0 0.1 copy.28
  26.1 0.1 reshape.259
  26.2 0.2 fusion.8
  26.4 1.4 scatter_custom_fusion
  27.8 0.7 all_to_all.14
  28.5 16.5 %all-to-all-start = ((s32[128,1,8]{2,1,0:T(1,128)}), s32[128,1,8]{2,1,0:T(1,128)S(1)}, u32[]{:S(2)}, u32[]{:S(2)}) async-start(s32[128,1,8]{2,1,0:T(1,128)} %bitcast.11), calls=%async_computation.1 | async-start | bytes 131072 | tf_op jit(solution)/shard_map/all_to_all | solution.py:77
  45.0 7.0 %maximum_convert_fusion = f32[8,288,1024]{2,1,0:T(8,128)} fusion(bf16[8,256,1024]{2,1,0:T(8,128)(2,1)} %bitcast.78, bf16[8,32,1024]{2,1,0:T(8,128)(2,1)S(1)} %bitcast.85), kind=kLoop, calls=%fused_computation.9 | loop fusion | flops 9437184 | bytes 14155776 | tf_op jit(solution)/shard_map/convert_element_type | solution.py:29
  52.1 3.8 all-to-all-done
  55.9 0.1 reshape.241
  56.0 78.8 %reduce-scatter.2.cloned.1.call-done = f32[288,1024]{1,0:T(8,128)} async-done(((f32[2304,1024]{1,0:T(8,128)}), f32[288,1024]{1,0:T(8,128)}) %reduce-scatter.2.cloned.1.call-update) | async-done | bytes 1179664 | tf_op jit(solution)/shard_map/reduce_scatter | solution.py:36
  134.7 1.8 add_convert_fusion
  136.5 0.0 copy-start.6
  136.5 0.7 multiply_reduce_fusion.1
  137.3 0.0 copy-start.10
  137.3 1.1 fusion.29
  138.4 0.8 copy-done.3
  139.2 0.0 copy-start.9
  139.2 5.2 %gather_fusion.1 = bf16[1024,768]{1,0:T(8,128)(2,1)} fusion(bf16[256,768]{1,0:T(8,128)(2,1)S(1)} %slice.60, s32[1024]{0:T(1024)S(1)} %broadcast_clamp_fusion), kind=kCustom, calls=%fused_computation.1 | custom fusion | bytes 3149824 | tf_op jit(solution)/shard_map/gather | solution.py:76
  144.4 11.2 %all-to-all-start.1 = ((bf16[128,8,768]{2,1,0:T(8,128)(2,1)}), bf16[128,8,768]{2,1,0:T(8,128)(2,1)S(1)}, u32[]{:S(2)}, u32[]{:S(2)}) async-start(bf16[128,8,768]{2,1,0:T(8,128)(2,1)} %bitcast.82), calls=%async_computation.2 | async-start | bytes 3145728 | tf_op jit(solution)/shard_map/all_to_all | solution.py:75
  155.6 0.0 all-reduce.3.cloned.1.call-start
  155.7 0.6 fusion.20
  156.3 1.9 reduce-window.16
  158.2 0.7 compare_select_fusion.3
  158.8 0.0 slice-start
  158.9 1.2 gather_fusion
  160.1 0.9 copy.30
  161.1 0.8 slice_bitcast_fusion
  161.9 35.5 %all-to-all-done.1 = bf16[128,8,768]{2,1,0:T(8,128)(2,1)S(1)} async-done(((bf16[128,8,768]{2,1,0:T(8,128)(2,1)}), bf16[128,8,768]{2,1,0:T(8,128)(2,1)S(1)}, u32[]{:S(2)}, u32[]{:S(2)}) %all-to-all-start.1) | async-done | bytes 1572896 | tf_op jit(solution)/shard_map/all_to_all | solution.py:75
  197.3 1.9 gather_fusion.2
  199.3 1.5 fusion.4
  200.7 0.1 copy.33
  200.9 0.1 copy.34
  201.0 1.4 fusion.3
  202.3 1.0 multiply_reduce_fusion.2
  203.4 3.2 fusion.12
  206.6 0.0 all-reduce.3.cloned.1.call-update
  206.6 0.2 slice_reduce_fusion
  206.8 0.1 fusion.19
  207.0 2.6 scatter_custom_fusion.1
  209.6 6.1 %all-to-all-start.2 = ((bf16[32,16,768]{2,1,0:T(8,128)(2,1)}), bf16[32,16,768]{2,1,0:T(8,128)(2,1)S(1)}, u32[]{:S(2)}, u32[]{:S(2)}) async-start(bf16[32,16,768]{2,1,0:T(8,128)(2,1)} %bitcast.23), calls=%async_computation.3 | async-start | bytes 1572864 | tf_op jit(solution)/shard_map/all_to_all | solution.py:61
  215.6 14.5 %all-to-all-done.2 = bf16[32,16,768]{2,1,0:T(8,128)(2,1)S(1)} async-done(((bf16[32,16,768]{2,1,0:T(8,128)(2,1)}), bf16[32,16,768]{2,1,0:T(8,128)(2,1)S(1)}, u32[]{:S(2)}, u32[]{:S(2)}) %all-to-all-start.2) | async-done | bytes 786464 | tf_op jit(solution)/shard_map/all_to_all | solution.py:61
  230.1 0.5 fusion.23
  230.7 236.0 %all-reduce.3.cloned.1.call-done = f32[1024,768]{1,0:T(8,128)} async-done(((f32[1024,768]{1,0:T(8,128)}), f32[1024,768]{1,0:T(8,128)}) %all-reduce.3.cloned.1.call-update) | async-done | bytes 3145744
  466.6 1.3 constant_dynamic-slice_fusion
  468.0 0.9 copy.49
  (42 shorter events, 0.3 us)
Async XLA Ops:
  7.2 129.4 %copy-start = (bf16[1024,768]{1,0:T(8,128)(2,1)S(1)}, bf16[1024,768]{1,0:T(8,128)(2,1)}, u32[]{:S(2)}) copy-start(bf16[1024,768]{1,0:T(8,128)(2,1)} %param.15) | copy-start | bytes 4718596
  7.2 5.7 %copy-start.2 = (bf16[256,1024]{1,0:T(8,128)(2,1)S(1)}, bf16[256,1024]{1,0:T(8,128)(2,1)}, u32[]{:S(2)}) copy-start(bf16[256,1024]{1,0:T(8,128)(2,1)} %param.10) | copy-start | bytes 1572868
  7.2 5.7 %copy-start.11 = (f32[1024]{0:T(1024)S(1)}, f32[1024]{0:T(1024)}, u32[]{:S(2)}) copy-start(f32[1024]{0:T(1024)} %param.12) | copy-start | bytes 12292
  7.2 127.5 %reduce-scatter.2.cloned.1.call-start = ((), (), s32[]{:S(2)}) async-start(), calls=%async_computation.4 | async-start | bytes 10616832 | tf_op jit(solution)/shard_map/reduce_scatter | solution.py:36
  7.2 5.7 %copy-start.1 = (bf16[2048,1024]{1,0:T(8,128)(2,1)S(1)}, bf16[2048,1024]{1,0:T(8,128)(2,1)}, u32[]{:S(2)}) copy-start(bf16[2048,1024]{1,0:T(8,128)(2,1)} %param.11) | copy-start | bytes 12582916
  14.2 5.1 %copy-start.13 = (bf16[512,1024]{1,0:T(8,128)(2,1)S(1)}, bf16[512,1024]{1,0:T(8,128)(2,1)}, u32[]{:S(2)}) copy-start(bf16[512,1024]{1,0:T(8,128)(2,1)} %param.14) | copy-start | bytes 3145732
  24.4 0.7 copy-start.8
  24.4 1.5 copy-start.12
  28.5 27.3 %all-to-all-start = ((s32[128,1,8]{2,1,0:T(1,128)}), s32[128,1,8]{2,1,0:T(1,128)S(1)}, u32[]{:S(2)}, u32[]{:S(2)}) async-start(s32[128,1,8]{2,1,0:T(1,128)} %bitcast.11), calls=%async_computation.1 | async-start | bytes 131072 | tf_op jit(solution)/shard_map/all_to_all | solution.py:77
  136.5 1.8 copy-start.6
  137.3 21.6 %copy-start.10 = (f32[288]{0:T(512)}, f32[288]{0:T(512)S(1)}, u32[]{:S(2)}) copy-start(f32[288]{0:T(512)S(1)} %add_sqrt_fusion) | copy-start | bytes 3460
  138.4 0.8 copy-start.3
  139.2 16.5 %copy-start.9 = (s32[256,1]{0,1:T(1,128)S(1)}, s32[256,1]{0,1:T(1,128)}, u32[]{:S(2)}) copy-start(s32[256,1]{0,1:T(1,128)} %param.19) | copy-start | bytes 3076
  144.4 52.9 %all-to-all-start.1 = ((bf16[128,8,768]{2,1,0:T(8,128)(2,1)}), bf16[128,8,768]{2,1,0:T(8,128)(2,1)S(1)}, u32[]{:S(2)}, u32[]{:S(2)}) async-start(bf16[128,8,768]{2,1,0:T(8,128)(2,1)} %bitcast.82), calls=%async_computation.2 | async-start | bytes 3145728 | tf_op jit(solution)/shard_map/all_to_all | solution.py:75
  155.6 311.0 %all-reduce.3.cloned.1.call-start = ((), (), s32[]{:S(2)}) async-start(), calls=%async_computation.5 | async-start | bytes 6291456
  158.8 44.5 %slice-start = ((f32[288]{0:T(512)}), f32[32]{0:T(128)S(1)}, s32[]{:S(2)}) async-start(f32[288]{0:T(512)} %copy-done.10), calls=%async_computation.6 | async-start | bytes 1024 | tf_op jit(solution)/shard_map/slice | solution.py:52
  160.1 42.2 %copy-start.5 = (bf16[32,768]{1,0:T(8,128)(2,1)S(1)}, bf16[32,768]{1,0:T(8,128)(2,1)}, u32[]{:S(2)}) copy-start(bf16[32,768]{1,0:T(8,128)(2,1)} %gather_fusion) | copy-start | bytes 147460
  199.3 7.4 %copy-start.7 = (s32[32,2,128]{2,0,1:T(8,128)S(1)}, s32[32,2,128]{2,0,1:T(8,128)}, u32[]{:S(2)}) copy-start(s32[32,2,128]{2,0,1:T(8,128)} %reduce-window.16) | copy-start | bytes 98308
  199.3 7.7 %copy-start.4 = (bf16[288,768]{1,0:T(8,128)(2,1)S(1)}, bf16[288,768]{1,0:T(8,128)(2,1)}, u32[]{:S(2)}) copy-start(bf16[288,768]{1,0:T(8,128)(2,1)} %copy-done.3) | copy-start | bytes 1327108
  209.6 20.6 %all-to-all-start.2 = ((bf16[32,16,768]{2,1,0:T(8,128)(2,1)}), bf16[32,16,768]{2,1,0:T(8,128)(2,1)S(1)}, u32[]{:S(2)}, u32[]{:S(2)}) async-start(bf16[32,16,768]{2,1,0:T(8,128)(2,1)} %bitcast.23), calls=%async_computation.3 | async-start | bytes 1572864 | tf_op jit(solution)/shard_map/all_to_all | solution.py:61
Sparse Core Ops, SparseCore 0:
  24.6 110.0 reduce-scatter.1
  206.7 259.8 all-reduce.2
where the time goes:
time: 477 us; the launch traced here: 476 us
  waiting for transfers between devices  369 us (77%)
  starting transfers between devices  33.9 us (7%)
  local copies, waits for them, and re-layouts  21.9 us (5%)
  other arithmetic  20 us (4%)
  matrix products  17 us (4%)
  between operations  14.4 us (3%)
    unnamed x3, waiting for transfers between devices  236 us
    reduce_scatter x1, waiting for transfers between devices, per_device(): lax.psum_scatter(jnp.dot(hidden, w_out, preferred_element_type=jnp.float3...  78.8 us
    all_to_all x1, waiting for transfers between devices, per_device(): lax.all_to_all(clip_embed[lax.all_to_all(wanted.reshape(peers, cap_fetch)...  35.5 us
    all_to_all x1, starting transfers between devices, per_device(): lax.all_to_all(wanted.reshape(peers, cap_fetch), ('dp', 'mp'), split_axis...  16.5 us
    all_to_all x1, waiting for transfers between devices, per_device(): lax.all_to_all(outgoing.reshape(owners, cap_index, embed_width), ('group'...  14.5 us
    all_to_all x1, starting transfers between devices, per_device(): lax.all_to_all(clip_embed[lax.all_to_all(wanted.reshape(peers, cap_fetch)...  11.2 us
  transfers between devices with their start and end apart: 5, of which 5 were waited for; matrix products, arithmetic and copies ran while one was open for 4% of the time, Pallas kernels for 0%

commit v1 on v0

--- a/solution.py
+++ b/solution.py
@@ -1,11 +1,213 @@
 import jax
 import jax.numpy as jnp
 from jax import lax
+from jax.experimental import pallas as pl
+from jax.experimental.pallas import tpu as pltpu
 from jax.sharding import PartitionSpec as P
 
 norm_eps = 1e-06
 embed_eps = 1e-06
 score_scale = 20.0
+MESH = pl.DeviceIdType.MESH
+f32 = jnp.float32
+bf16 = jnp.bfloat16
+
+
+def part_of(way, dist):
+    return 0 if dist == 4 else 7 - 2 * dist + way
+
+
+def encode_kernel(
+    q_hbm, c_hbm, gain_ref, win_hbm, wout_hbm, proj_hbm,
+    embc_ref, embq_ref, unitq_ref, lenq_ref, sumq_ref,
+    xq, xc, win, wout, proj, woutp, normed, hidden, cpart, qpart, base, crecv, qrecv,
+    load_sem, csend_sem, crecv_sem, qsend_sem, qrecv_sem,
+):
+    ring = 8
+    me = lax.axis_index("mp")
+    right, left = lax.rem(me + 1, ring), lax.rem(me + ring - 1, ring)
+
+    def home_of(i):
+        even = 8 - (8 - i) // 2
+        odd = (7 - i) // 2
+        return lax.rem(me + jnp.where(lax.rem(i, 2) == 0, even, odd), ring)
+
+    def load_x(i):
+        rows = pl.ds(pl.multiple_of(home_of(jnp.int32(i)) * 256, 256), 256)
+        return pltpu.make_async_copy(c_hbm.at[rows], xc.at[i], load_sem.at[i])
+
+    loads = [
+        pltpu.make_async_copy(q_hbm, xq, load_sem.at[8]),
+        pltpu.make_async_copy(win_hbm, win, load_sem.at[9]),
+        pltpu.make_async_copy(wout_hbm, wout, load_sem.at[10]),
+        pltpu.make_async_copy(proj_hbm, proj, load_sem.at[11]),
+    ]
+    for load in loads:
+        load.start()
+    for i in range(8):
+        load_x(i).start()
+
+    barrier = pltpu.get_barrier_semaphore()
+    for neighbour in (left, right):
+        pl.semaphore_signal(barrier, inc=1, device_id={"mp": neighbour}, device_id_type=MESH)
+
+    def normalise(src):
+        @pl.loop(0, 8)
+        def _(r):
+            rows = pl.ds(pl.multiple_of(r * 32, 32), 32)
+            v = src[rows, :].astype(f32)
+            scale = lax.rsqrt(jnp.mean(v * v, axis=-1, keepdims=True) + norm_eps)
+            normed[rows, :] = (v * scale * gain_ref[...]).astype(bf16)
+
+    def feed():
+        for n in range(2):
+            gate = jnp.dot(normed[...], win[:, n * 256:(n + 1) * 256], preferred_element_type=f32)
+            upper = jnp.dot(normed[...], win[:, 512 + n * 256:768 + n * 256], preferred_element_type=f32)
+            hidden[:, n * 256:(n + 1) * 256] = (gate / (1.0 + jnp.exp(-gate)) * upper).astype(bf16)
+
+    loads[0].wait()
+    normalise(xq)
+    loads[1].wait()
+    feed()
+    loads[2].wait()
+    mixed_q = jnp.dot(hidden[...], wout[...], preferred_element_type=f32).astype(bf16)
+    normed[...] = mixed_q
+    for i in range(8):
+        h = home_of(jnp.int32(i))
+        qpart[i] = normed[pl.ds(pl.multiple_of(h * 32, 32), 32), :]
+    loads[3].wait()
+    woutp[...] = jnp.dot(wout[...], proj[...], preferred_element_type=f32).astype(bf16)
+    pl.semaphore_wait(barrier, 2)
+
+    def copies(way, u):
+        first = way
+        if u == 0:
+            dist, half = 4, first
+        elif u % 2 == 1:
+            dist, half = 4 - (u + 1) // 2, 1 - first
+        else:
+            dist, half = 4 - u // 2, first
+        i = part_of(way, dist)
+        target = {"mp": right if way == 0 else left}
+        crows, qrows = pl.ds(half * 128, 128), pl.ds(half * 16, 16)
+        return (i, crows, qrows,
+            pltpu.make_async_remote_copy(
+                src_ref=cpart.at[i, crows], dst_ref=crecv.at[way, u], send_sem=csend_sem.at[way, u],
+                recv_sem=crecv_sem.at[way, u], device_id=target, device_id_type=MESH),
+            pltpu.make_async_remote_copy(
+                src_ref=qpart.at[i, qrows], dst_ref=qrecv.at[way, u], send_sem=qsend_sem.at[way, u],
+                recv_sem=qrecv_sem.at[way, u], device_id=target, device_id_type=MESH))
+
+    def unit(way, u):
+        i, crows, qrows, ccopy, qcopy = copies(way, u)
+        if u >= 2:
+            _, _, _, cbefore, qbefore = copies(way, u - 2)
+            qbefore.wait_recv()
+            qpart[i, qrows] = (qpart[i, qrows].astype(f32) + qrecv[way, u - 2].astype(f32)).astype(bf16)
+            cbefore.wait_recv()
+            cpart[i, crows] = (cpart[i, crows].astype(f32) + crecv[way, u - 2].astype(f32)).astype(bf16)
+        ccopy.start()
+        qcopy.start()
+
+    @pl.loop(0, 8)
+    def _(i):
+        load_x(i).wait()
+        normalise(xc.at[i])
+        feed()
+        cpart[i] = jnp.dot(hidden[...], woutp[...], preferred_element_type=f32).astype(bf16)
+
+        @pl.when(i == 0)
+        def _():
+            unit(0, 0)
+            unit(1, 0)
+
+        @pl.when(i == 1)
+        def _():
+            unit(0, 1)
+
+        @pl.when(i == 2)
+        def _():
+            unit(1, 1)
+
+        @pl.when(i == 4)
+        def _():
+            unit(0, 2)
+            unit(1, 2)
+
+    for u in (3, 4):
+        for way in (0, 1):
+            unit(way, u)
+    base[...] = jnp.dot(xc[7], proj[...], preferred_element_type=f32) + cpart[7].astype(f32)
+    for u in (5, 6):
+        for way in (0, 1):
+            unit(way, u)
+
+    for way in (0, 1):
+        for u in (5, 6):
+            _, _, _, ccopy, qcopy = copies(way, u)
+            qcopy.wait_recv()
+            ccopy.wait_recv()
+    for half in range(2):
+        ua, ub = (6, 5) if half == 0 else (5, 6)
+        for r in range(0, 128, 64):
+            rows = slice(half * 128 + r, half * 128 + r + 64)
+            raw = base[rows, :] + crecv[0, ua, r:r + 64, :].astype(f32) + crecv[1, ub, r:r + 64, :].astype(f32)
+            inverse = lax.rsqrt(jnp.sum(raw * raw, axis=-1, keepdims=True) + embed_eps)
+            embc_ref[rows, :] = (raw * inverse).astype(bf16)
+        qrows = slice(half * 16, half * 16 + 16)
+        own = xq[pl.ds(pl.multiple_of(me * 32 + half * 16, 16), 16), :].astype(f32)
+        mixed = qpart[7, qrows, :].astype(f32) + qrecv[0, ua].astype(f32) + qrecv[1, ub].astype(f32)
+        sumq_ref[qrows, :] = (own + mixed).astype(bf16)
+    raw_q = jnp.dot(sumq_ref[...], proj[...], preferred_element_type=f32)
+    length = jnp.sqrt(jnp.sum(raw_q * raw_q, axis=-1, keepdims=True) + embed_eps)
+    unit_q = raw_q / length
+    unitq_ref[...] = unit_q
+    embq_ref[...] = unit_q.astype(bf16)
+    lenq_ref[...] = jnp.broadcast_to(length, (32, 128))
+    for way in (0, 1):
+        for u in range(7):
+            _, _, _, ccopy, qcopy = copies(way, u)
+            ccopy.wait_send()
+            qcopy.wait_send()
+
+
+def encode(queries, clips, gain, win, wout, proj):
+    any_spec = pl.BlockSpec(memory_space=pl.ANY)
+    vmem = pl.BlockSpec(memory_space=pltpu.VMEM)
+    sds = jax.ShapeDtypeStruct
+    return pl.pallas_call(
+        encode_kernel,
+        out_shape=(
+            sds((256, 768), bf16), sds((32, 768), bf16), sds((32, 768), f32), sds((32, 128), f32),
+            sds((32, 1024), bf16),
+        ),
+        in_specs=[any_spec, any_spec, vmem, any_spec, any_spec, any_spec],
+        out_specs=[vmem] * 5,
+        scratch_shapes=[
+            pltpu.VMEM((256, 1024), bf16),
+            pltpu.VMEM((8, 256, 1024), bf16),
+            pltpu.VMEM((1024, 1024), bf16),
+            pltpu.VMEM((512, 1024), bf16),
+            pltpu.VMEM((1024, 768), bf16),
+            pltpu.VMEM((512, 768), bf16),
+            pltpu.VMEM((256, 1024), bf16),
+            pltpu.VMEM((256, 512), bf16),
+            pltpu.VMEM((8, 256, 768), bf16),
+            pltpu.VMEM((8, 32, 1024), bf16),
+            pltpu.VMEM((256, 768), f32),
+            pltpu.VMEM((2, 7, 128, 768), bf16),
+            pltpu.VMEM((2, 7, 16, 1024), bf16),
+            pltpu.SemaphoreType.DMA((12,)),
+            pltpu.SemaphoreType.DMA((2, 7)),
+            pltpu.SemaphoreType.DMA((2, 7)),
+            pltpu.SemaphoreType.DMA((2, 7)),
+            pltpu.SemaphoreType.DMA((2, 7)),
+        ],
+        compiler_params=pltpu.CompilerParams(
+            collective_id=0, has_side_effects=True, vmem_limit_bytes=48 * 1024 * 1024),
+        cost_estimate=pl.CostEstimate(flops=8_500_000_000, bytes_accessed=20_000_000, transcendentals=2_000_000),
+        name="encode",
+    )(queries, clips, gain, win, wout, proj)
 
 
 def slots_of(owner_ids, owners):
@@ -16,41 +218,13 @@
 def per_device(
     queries, clips, norm_gain, w_in, w_out, proj, pos_row, neg_owner, neg_row, clip_dest
 ):
-    slices = lax.axis_size("mp")
-    query_total, width = queries.shape
-    query_rows = query_total // slices
-    clip_rows = clips.shape[0] // slices
-    per_block = query_rows + clip_rows
-    hidden_local = w_out.shape[0]
-    stacked = jnp.concatenate(
-        [queries.reshape(slices, query_rows, width), clips.reshape(slices, clip_rows, width)],
-        axis=1,
-    ).reshape(slices * per_block, width)
-    values = stacked.astype(jnp.float32)
-    scale = lax.rsqrt(jnp.mean(values * values, axis=-1, keepdims=True) + norm_eps)
-    normed = (values * scale * norm_gain).astype(jnp.bfloat16)
-    start_row = lax.axis_index("mp") * per_block
-    merged = w_in.reshape(width, 2 * hidden_local)
-    both = jnp.dot(normed, merged, preferred_element_type=jnp.float32)
-    hidden = (jax.nn.silu(both[:, :hidden_local]) * both[:, hidden_local:]).astype(jnp.bfloat16)
-    mixed = lax.psum_scatter(
-        jnp.dot(hidden, w_out, preferred_element_type=jnp.float32),
-        "mp",
-        scatter_dimension=0,
-        tiled=True,
-    )
-    residual = lax.dynamic_slice_in_dim(values, start_row, per_block, 0)
-    summed = (residual + mixed).astype(jnp.bfloat16)
-    raw = jnp.dot(summed, proj, preferred_element_type=jnp.float32)
-    length = jnp.sqrt(jnp.sum(raw * raw, axis=-1, keepdims=True) + embed_eps)
-    unit = raw / length
-    embedded = unit.astype(jnp.bfloat16)
-    embed_width = embedded.shape[1]
-    query_embed = embedded[:query_rows]
-    clip_embed = embedded[query_rows:]
-    query_unit = unit[:query_rows]
-    query_length = length[:query_rows]
-    query_summed = summed[:query_rows]
+    width = queries.shape[1]
+    query_rows = pos_row.shape[0]
+    clip_rows = clip_dest.shape[0]
+    clip_embed, query_embed, query_unit, query_length, query_summed = encode(
+        queries, clips, norm_gain.reshape(1, width), w_in.reshape(width, -1), w_out, proj)
+    query_length = query_length[:, :1]
+    embed_width = clip_embed.shape[1]
     owners = lax.axis_size(("group", "dp"))
     destination = clip_dest[:, 0]
     cap_index = max(2, min(clip_rows, 2 * clip_rows // owners))
@@ -102,10 +276,17 @@
     dunit = score_scale * (jnp.einsum("qc,qce->qe", probs, candidates) - candidates[:, 0, :])
     along = jnp.sum(query_unit * dunit, axis=-1, keepdims=True)
     draw = ((dunit - query_unit * along) / query_length).astype(jnp.bfloat16)
+    slices = lax.axis_size("mp")
+    pieces = query_summed.reshape(query_rows, owners, slices, -1).transpose(2, 0, 1, 3)
+    pieces = lax.all_to_all(
+        pieces.reshape(slices, query_rows, -1), "mp", split_axis=0, concat_axis=0, tiled=True)
+    draws = lax.all_gather(draw, "mp", axis=0, tiled=True)
     term = lax.dot_general(
-        query_summed, draw, (((0,), (0,)), ((), ())), preferred_element_type=jnp.float32
-    )
-    grad_proj = lax.psum_scatter(term, ("group", "dp", "mp"), scatter_dimension=0, tiled=True)
+        pieces.reshape(slices * query_rows, -1), draws, (((0,), (0,)), ((), ())),
+        preferred_element_type=jnp.float32)
+    shares = lax.all_to_all(
+        term.reshape(owners, -1, embed_width), ("group", "dp"), split_axis=0, concat_axis=0, tiled=True)
+    grad_proj = jnp.sum(shares, axis=0)
     return (losses, index_shard, grad_proj)
 
 

time: 477 us -> 189 us (0.40)
  waiting for transfers between devices: 369 us -> 46.2 us
  Pallas kernels: 0 us -> 43.3 us
  blocking collectives: 0 us -> 20 us
  starting transfers between devices: 33.9 us -> 53.3 us
  other arithmetic: 20 us -> 3.37 us
  matrix products: 17 us -> 0.97 us
  between operations: 14.4 us -> 0.93 us
    unnamed x3 -> x0, waiting for transfers between devices: 236 us -> none
    reduce_scatter x1 -> x0, waiting for transfers between devices: 78.8 us -> none  [per_device(): lax.psum_scatter(jnp.dot(hidden, w_out, preferred_element_type=jnp.float3...]
    pallas_call x0 -> x1, Pallas kernels: none -> 43.3 us  [encode(): pl.pallas_call(encode_kernel, out_shape=(sds((256, 768), bf16), sds((32,...]
    all_gather x0 -> x1, blocking collectives: none -> 20 us  [per_device(): draws = lax.all_gather(draw, 'mp', axis=0, tiled=True)]
    all_to_all x0 -> x2, starting transfers between devices: none -> 16.7 us  [the longest x1 12.4 us: per_device(): lax.all_to_all(term.reshape(owners, -1, embed_width), ('group', 'dp'), sp...]
    all_to_all x1, waiting for transfers between devices: 14.5 us -> 0.01 us  [per_device(): lax.all_to_all(outgoing.reshape(owners, cap_index, embed_width), ('group'...]
    dot_general x4 -> x1, matrix products: 14.2 us -> 0.21 us  [per_device(): lax.dot_general(pieces.reshape(slices * query_rows, -1), draws, (((0,), (...]
    convert_element_type x4 -> x1, other arithmetic: 11.1 us -> 0.09 us  [per_device(): draw = ((dunit - query_unit * along) / query_length).astype(jnp.bfloat16)]
  transfers between devices with their start and end apart: 5 -> 5, of which waited for: 5 -> 3; matrix products, arithmetic and copies ran while one was open for 4% -> 9% of each run, Pallas kernels for 0% -> 23%
where the time goes in v1:
time: 189 us; the launch traced here: 188 us
  starting transfers between devices  53.3 us (28%)
  waiting for transfers between devices  46.2 us (24%)
  Pallas kernels  43.3 us (23%)
  blocking collectives  20 us (11%)
  local copies, waits for them, and re-layouts  19.9 us (11%)
  other arithmetic  3.37 us (2%)
    pallas_call x1, Pallas kernels, encode(): pl.pallas_call(encode_kernel, out_shape=(sds((256, 768), bf16), sds((32,...  43.3 us
    all_to_all x1, waiting for transfers between devices, per_device(): lax.all_to_all(clip_embed[lax.all_to_all(wanted.reshape(peers, cap_fetch)...  35.3 us
    all_gather x1, blocking collectives, per_device(): draws = lax.all_gather(draw, 'mp', axis=0, tiled=True)  20 us
    all_to_all x1, starting transfers between devices, per_device(): lax.all_to_all(wanted.reshape(peers, cap_fetch), ('dp', 'mp'), split_axis...  16.3 us
    all_to_all x1, starting transfers between devices, per_device(): lax.all_to_all(clip_embed[lax.all_to_all(wanted.reshape(peers, cap_fetch)...  12.6 us
    all_to_all x1, starting transfers between devices, per_device(): lax.all_to_all(term.reshape(owners, -1, embed_width), ('group', 'dp'), sp...  12.4 us
    all_to_all x1, waiting for transfers between devices, per_device(): lax.all_to_all(term.reshape(owners, -1, embed_width), ('group', 'dp'), sp...  9.02 us
    all_to_all x1, starting transfers between devices, per_device(): lax.all_to_all(outgoing.reshape(owners, cap_index, embed_width), ('group'...  7.71 us
  transfers between devices with their start and end apart: 5, of which 3 were waited for; matrix products, arithmetic and copies ran while one was open for 9% of the time, Pallas kernels for 23%

profile of v1, /device:TPU:1, one launch (start us, length us, event | category | flops | bytes accessed | tf_op | source)
XLA Modules:
  0.0 187.9 jit_solution(14713947667869718357)
XLA Ops:
  0.6 0.8 copy.40
  1.4 0.1 eq.54
  1.5 0.1 eq.50
  1.6 0.7 broadcast_multiply_fusion
  2.3 0.1 copy.42
  2.4 0.2 fusion.6
  2.7 0.2 fusion.7
  2.9 0.1 copy.39
  2.9 0.1 mul.54
  3.0 0.8 copy.44
  3.8 0.1 reshape.189
  3.9 1.4 scatter_custom_fusion
  5.3 0.7 all_to_all.20
  6.0 16.3 %all-to-all-start = ((s32[128,1,8]{2,1,0:T(1,128)}), s32[128,1,8]{2,1,0:T(1,128)S(1)}, u32[]{:S(2)}, u32[]{:S(2)}) async-start(s32[128,1,8]{2,1,0:T(1,128)} %bitcast.8), calls=%async_computation | async-start | bytes 131072 | tf_op jit(solution)/shard_map/all_to_all | solution.py:251
  22.4 0.0 copy-start
  22.4 0.0 copy-start.1
  22.4 0.0 copy-start.2
  22.4 0.0 copy-start.3
  22.4 2.3 %copy.59 = bf16[128,8,2,512]{3,1,2,0:T(8,128)(2,1)S(1)} copy(bf16[128,8,2,512]{3,2,1,0:T(2,128)(2,1)} %bitcast.84) | data formatting | bytes 4194304
  24.7 0.0 copy-done
  24.8 0.0 copy-done.1
  24.8 0.1 copy-done.2
  24.8 0.0 copy-done.3
  24.8 43.3 %encode.1 = (bf16[256,768]{1,0:T(8,128)(2,1)S(1)}, bf16[32,768]{1,0:T(8,128)(2,1)S(1)}, f32[32,768]{1,0:T(8,128)S(1)}, f32[32,128]{1,0:T(8,128)S(1)}, bf16[32,1024]{1,0:T(8,128)(2,1)S(1)}) custom-call(bf16[256,1024]{1,0:T(8,128)(2,1)S(1)} %copy-done.2, bf16[2048,1024]{1,0:T(8,128)(2,1)} %c_hbm.1, f32[1,1024]{1,0:T(1,128)S(1)} %bitcast.78, ...), custom_call_target="tpu_custom_call" | custom-call | flops 8499999744 | bytes 20000000 | tf_op jit(solution)/shard_map/encode/pallas_call | solution.py:178
  68.1 0.2 copy.48
  68.3 0.8 copy.50
  69.1 0.0 all-to-all-done
  69.1 4.3 %all-to-all-start.3 = ((bf16[8,32,128]{2,1,0:T(8,128)(2,1)}), bf16[8,32,128]{2,1,0:T(8,128)(2,1)S(1)}, u32[]{:S(2)}, u32[]{:S(2)}) async-start(bf16[8,32,128]{2,1,0:T(8,128)(2,1)} %copy.50), calls=%async_computation.3 | async-start | bytes 131072 | tf_op jit(solution)/shard_map/all_to_all | solution.py:281
  73.4 0.1 reshape.171
  73.5 5.2 %gather_fusion.1 = bf16[1024,768]{1,0:T(8,128)(2,1)} fusion(bf16[256,768]{1,0:T(8,128)(2,1)S(1)} %get-tuple-element.9, s32[1024]{0:T(1024)S(1)} %broadcast_clamp_fusion), kind=kCustom, calls=%fused_computation.1 | custom fusion | bytes 3149824 | tf_op jit(solution)/shard_map/gather | solution.py:250
  78.7 1.9 %all-to-all-done.3 = bf16[8,32,128]{2,1,0:T(8,128)(2,1)S(1)} async-done(((bf16[8,32,128]{2,1,0:T(8,128)(2,1)}), bf16[8,32,128]{2,1,0:T(8,128)(2,1)S(1)}, u32[]{:S(2)}, u32[]{:S(2)}) %all-to-all-start.3) | async-done | bytes 65568 | tf_op jit(solution)/shard_map/all_to_all | solution.py:281
  80.6 0.0 copy-start.5
  80.6 0.0 copy-start.4
  80.6 12.6 %all-to-all-start.1 = ((bf16[128,8,768]{2,1,0:T(8,128)(2,1)}), bf16[128,8,768]{2,1,0:T(8,128)(2,1)S(1)}, u32[]{:S(2)}, u32[]{:S(2)}) async-start(bf16[128,8,768]{2,1,0:T(8,128)(2,1)} %bitcast.81), calls=%async_computation.1 | async-start | bytes 3145728 | tf_op jit(solution)/shard_map/all_to_all | solution.py:249
  93.2 0.0 copy-done.5
  93.2 0.6 gather_fusion
  93.9 0.1 copy.46
  94.0 0.0 copy-done.4
  94.0 0.6 reduce-window.16
  94.6 0.2 slice_reduce_fusion
  94.8 0.1 fusion.14
  94.9 2.6 %scatter_custom_fusion.1 = bf16[512,768]{1,0:T(8,128)(2,1)} fusion(s32[256]{0:T(256)S(1)} %bitcast.101, bf16[256,768]{1,0:T(8,128)(2,1)S(1)} %get-tuple-element.9, bf16[]{:T(256)} %constant.8.clone.1), kind=kCustom, calls=%fused_computation.10 | custom fusion | bytes 786434 | tf_op jit(solution)/shard_map/scatter | solution.py:233
  97.5 0.1 slice_reduce_fusion.1
  97.6 0.1 copy.51
  97.8 35.3 %all-to-all-done.1 = bf16[128,8,768]{2,1,0:T(8,128)(2,1)S(1)} async-done(((bf16[128,8,768]{2,1,0:T(8,128)(2,1)}), bf16[128,8,768]{2,1,0:T(8,128)(2,1)S(1)}, u32[]{:S(2)}, u32[]{:S(2)}) %all-to-all-start.1) | async-done | bytes 1572896 | tf_op jit(solution)/shard_map/all_to_all | solution.py:249
  133.1 7.7 %all-to-all-start.2 = ((bf16[32,16,768]{2,1,0:T(8,128)(2,1)}), bf16[32,16,768]{2,1,0:T(8,128)(2,1)S(1)}, u32[]{:S(2)}, u32[]{:S(2)}) async-start(bf16[32,16,768]{2,1,0:T(8,128)(2,1)} %bitcast.83), calls=%async_computation.2 | async-start | bytes 1572864 | tf_op jit(solution)/shard_map/all_to_all | solution.py:235
  140.8 1.2 gather_fusion.2
  142.0 0.4 fusion.1
  142.4 0.1 copy.55
  142.6 0.1 copy.56
  142.7 0.4 fusion
  143.0 0.1 multiply_reduce_fusion
  143.2 0.1 divide_convert_fusion
  143.2 20.0 %all_gather.3 = bf16[256,768]{1,0:T(8,128)(2,1)S(1)} all-gather(bf16[32,768]{1,0:T(8,128)(2,1)S(1)} %divide_convert_fusion), channel_id=1, replica_groups=mesh['group'=2,'dp'=16,'mp'=8] {'mp'}, dimensions={0}, use_global_device_ids=true | all-gather | bytes 442368 | tf_op jit(solution)/shard_map/all_gather | solution.py:283
  163.2 0.2 fusion.2
  163.4 1.0 copy.53
  164.4 0.0 all-to-all-done.2
  164.4 12.4 %all-to-all-start.4 = ((f32[32,4,768]{2,1,0:T(4,128)}), f32[32,4,768]{2,1,0:T(4,128)S(1)}, u32[]{:S(2)}, u32[]{:S(2)}) async-start(f32[32,4,768]{2,1,0:T(4,128)} %copy.53), calls=%async_computation.4 | async-start | bytes 786432 | tf_op jit(solution)/shard_map/all_to_all | solution.py:287
  176.8 0.5 fusion.18
  177.3 9.0 %all-to-all-done.4 = f32[32,4,768]{2,1,0:T(4,128)S(1)} async-done(((f32[32,4,768]{2,1,0:T(4,128)}), f32[32,4,768]{2,1,0:T(4,128)S(1)}, u32[]{:S(2)}, u32[]{:S(2)}) %all-to-all-start.4) | async-done | bytes 393248 | tf_op jit(solution)/shard_map/all_to_all | solution.py:287
  186.4 0.7 reduce_sum.49
  187.0 0.9 copy.71
  (22 shorter events, 0.3 us)
Async XLA Ops:
  6.0 63.1 %all-to-all-start = ((s32[128,1,8]{2,1,0:T(1,128)}), s32[128,1,8]{2,1,0:T(1,128)S(1)}, u32[]{:S(2)}, u32[]{:S(2)}) async-start(s32[128,1,8]{2,1,0:T(1,128)} %bitcast.8), calls=%async_computation | async-start | bytes 131072 | tf_op jit(solution)/shard_map/all_to_all | solution.py:251
  22.4 2.4 %copy-start = (bf16[1024,768]{1,0:T(8,128)(2,1)S(1)}, bf16[1024,768]{1,0:T(8,128)(2,1)}, u32[]{:S(2)}) copy-start(bf16[1024,768]{1,0:T(8,128)(2,1)} %proj_hbm.1) | copy-start | bytes 4718596
  22.4 2.4 %copy-start.1 = (bf16[512,1024]{1,0:T(8,128)(2,1)S(1)}, bf16[512,1024]{1,0:T(8,128)(2,1)}, u32[]{:S(2)}) copy-start(bf16[512,1024]{1,0:T(8,128)(2,1)} %wout_hbm.1) | copy-start | bytes 3145732
  22.4 2.4 %copy-start.2 = (bf16[256,1024]{1,0:T(8,128)(2,1)S(1)}, bf16[256,1024]{1,0:T(8,128)(2,1)}, u32[]{:S(2)}) copy-start(bf16[256,1024]{1,0:T(8,128)(2,1)} %q_hbm.1) | copy-start | bytes 1572868
  22.4 2.4 %copy-start.3 = (f32[1024]{0:T(1024)S(1)}, f32[1024]{0:T(1024)}, u32[]{:S(2)}) copy-start(f32[1024]{0:T(1024)} %param.12) | copy-start | bytes 12292
  69.1 11.5 %all-to-all-start.3 = ((bf16[8,32,128]{2,1,0:T(8,128)(2,1)}), bf16[8,32,128]{2,1,0:T(8,128)(2,1)S(1)}, u32[]{:S(2)}, u32[]{:S(2)}) async-start(bf16[8,32,128]{2,1,0:T(8,128)(2,1)} %copy.50), calls=%async_computation.3 | async-start | bytes 131072 | tf_op jit(solution)/shard_map/all_to_all | solution.py:281
  80.6 12.6 %copy-start.5 = (s32[32]{0:T(128)S(1)}, s32[32]{0:T(128)}, u32[]{:S(2)}) copy-start(s32[32]{0:T(128)} %param.16) | copy-start | bytes 388
  80.6 13.3 %copy-start.4 = (s32[256,1]{0,1:T(1,128)S(1)}, s32[256,1]{0,1:T(1,128)}, u32[]{:S(2)}) copy-start(s32[256,1]{0,1:T(1,128)} %param.19) | copy-start | bytes 3076
  80.6 52.5 %all-to-all-start.1 = ((bf16[128,8,768]{2,1,0:T(8,128)(2,1)}), bf16[128,8,768]{2,1,0:T(8,128)(2,1)S(1)}, u32[]{:S(2)}, u32[]{:S(2)}) async-start(bf16[128,8,768]{2,1,0:T(8,128)(2,1)} %bitcast.81), calls=%async_computation.1 | async-start | bytes 3145728 | tf_op jit(solution)/shard_map/all_to_all | solution.py:249
  133.1 31.3 %all-to-all-start.2 = ((bf16[32,16,768]{2,1,0:T(8,128)(2,1)}), bf16[32,16,768]{2,1,0:T(8,128)(2,1)S(1)}, u32[]{:S(2)}, u32[]{:S(2)}) async-start(bf16[32,16,768]{2,1,0:T(8,128)(2,1)} %bitcast.83), calls=%async_computation.2 | async-start | bytes 1572864 | tf_op jit(solution)/shard_map/all_to_all | solution.py:235
  164.4 21.9 %all-to-all-start.4 = ((f32[32,4,768]{2,1,0:T(4,128)}), f32[32,4,768]{2,1,0:T(4,128)S(1)}, u32[]{:S(2)}, u32[]{:S(2)}) async-start(f32[32,4,768]{2,1,0:T(4,128)} %copy.53), calls=%async_computation.4 | async-start | bytes 786432 | tf_op jit(solution)/shard_map/all_to_all | solution.py:287

commit v2 on v1

--- a/solution.py
+++ b/solution.py
@@ -210,84 +210,307 @@
     )(queries, clips, gain, win, wout, proj)
 
 
-def slots_of(owner_ids, owners):
-    onehot = (owner_ids[:, None] == jnp.arange(owners, dtype=jnp.int32)[None, :]).astype(jnp.int32)
-    return jnp.sum(jnp.cumsum(onehot, axis=0) * onehot, axis=-1) - 1
+def exchange_kernel(
+    embc_ref, embq_ref, unitq_ref, lenq_ref, sumq_ref, codes_ref, column_ref, idx_ref, pos_ref,
+    loss_ref, grad_ref, index_ref,
+    fetch, cands, qall, packed, slots, pieces, pieces_in, sums, sums_in, draw, draws, gshare, gshare_in,
+    fetch_s, fetch_r, q_s, q_r, piece_s, piece_r, idx_s, idx_r, sums_s, sums_r, draw_s, draw_r, grad_s, grad_r,
+):
+    g, d, z = lax.axis_index("group"), lax.axis_index("dp"), lax.axis_index("mp")
+    here = g * 16 + d
+
+    def up(s):
+        return lax.rem(z + s, 8)
+
+    def across(s):
+        return lax.rem(d + s, 16)
+
+    def beyond(s):
+        return lax.rem(here + s, 32)
+
+    def plane(o):
+        return {"group": o // 16, "dp": lax.rem(o, 16)}
+
+    barrier = pltpu.get_barrier_semaphore()
+
+    @pl.loop(1, 32)
+    def _(s):
+        pl.semaphore_signal(barrier, inc=1, device_id=plane(beyond(s)), device_id_type=MESH)
+
+    @pl.loop(1, 8)
+    def _(s):
+        pl.semaphore_signal(barrier, inc=1, device_id={"mp": up(s)}, device_id_type=MESH)
+
+    def remote(src, dst, send, recv, target):
+        return pltpu.make_async_remote_copy(
+            src_ref=src, dst_ref=dst, send_sem=send, recv_sem=recv, device_id=target, device_id_type=MESH)
+
+    def q_copy(to, frm):
+        return remote(embq_ref, qall.at[frm], q_s.at[to], q_r.at[frm], {"mp": to})
+
+    def fetch_copy(to, frm):
+        return remote(fetch.at[to], cands.at[:, frm], fetch_s.at[to], fetch_r.at[frm], {"dp": to})
+
+    def piece_copy(to, frm):
+        return remote(pieces.at[to], pieces_in.at[frm], piece_s.at[to], piece_r.at[frm], {"mp": to})
+
+    def index_copy(to, frm):
+        return remote(slots.at[to], index_ref.at[frm], idx_s.at[to], idx_r.at[frm], plane(to))
+
+    def sums_copy(to, frm):
+        return remote(sums.at[to], sums_in.at[frm], sums_s.at[to], sums_r.at[frm], {"mp": to})
+
+    def draw_copy(to, frm):
+        return remote(draw, draws.at[frm], draw_s.at[to], draw_r.at[frm], {"mp": to})
+
+    def grad_copy(to, frm):
+        return remote(gshare.at[to], gshare_in.at[frm], grad_s.at[to], grad_r.at[frm], plane(to))
+
+    owner_slot = (d * 8 + z) * 8
+
+    def pack(block):
+        rank = lax.broadcasted_iota(jnp.int32, (8, 256), 0)
+        for n in range(32):
+            code = codes_ref[pl.ds(block * 32 + n, 1), :]
+            hit = (code >> 8) == owner_slot + rank
+            row = jnp.sum(jnp.where(hit, (code & 255) + 1, 0), axis=1, keepdims=True) - 1
+            spot = lax.broadcasted_iota(jnp.int32, (8, 256), 1)
+            packed[n * 8:(n + 1) * 8, :] = jnp.where(spot == row, 1.0, 0.0)
+        rows = jnp.dot(packed[...].astype(bf16), embc_ref[...], preferred_element_type=f32).astype(bf16)
+        for c in range(4):
+            for part in range(4):
+                fetch[block * 4 + c, part] = rows[c * 64 + part * 16:c * 64 + part * 16 + 16]
+
+    y = d // 4
+    pack(lax.rem(y + 1, 4))
+    pl.semaphore_wait(barrier, 38)
+
+    @pl.loop(1, 8)
+    def _(s):
+        q_copy(up(s), z).start()
+
+    qall[z] = embq_ref[...]
+
+    @pl.loop(0, 4)
+    def _(s):
+        block = lax.rem(y + 1 + s, 4)
+
+        @pl.when(s > 0)
+        def _():
+            pack(block)
+
+        @pl.loop(0, 4)
+        def _(c):
+            to = block * 4 + c
+
+            @pl.when(to != d)
+            def _():
+                fetch_copy(to, d).start()
+
+    cands[:, d] = fetch[d]
+
+    @pl.loop(0, 2)
+    def _(s):
+        row = lax.broadcasted_iota(jnp.int32, (256, 256), 0) + s * 256
+        onehot = jnp.where(row == idx_ref[...], 1.0, 0.0).astype(bf16)
+        rows = jnp.dot(onehot, embc_ref[...], preferred_element_type=f32).astype(bf16)
+        slots[pl.ds(s * 16, 16)] = rows.reshape(16, 16, 768)
+
+    @pl.loop(0, 8)
+    def _(s):
+        m = up(s)
+        source = lax.broadcasted_iota(jnp.int32, (1024, 256), 0)
+        lane = lax.broadcasted_iota(jnp.int32, (1024, 256), 1)
+        onehot = jnp.where(source == (lane >> 3) * 32 + m * 4 + (lane & 3), 1.0, 0.0).astype(bf16)
+        pieces[m] = jnp.dot(sumq_ref[...], onehot, preferred_element_type=f32).astype(bf16)
+
+        @pl.when(s > 0)
+        def _():
+            piece_copy(m, z).start()
+
+    pieces_in[z] = pieces[z]
+    unit = unitq_ref[...]
+    length = lenq_ref[:, 0:1]
+    at_pos = lax.broadcasted_iota(jnp.int32, (32, 256), 1) == pos_ref[...]
+    positive = jnp.dot(
+        jnp.where(at_pos, 1.0, 0.0).astype(bf16), embc_ref[...], preferred_element_type=f32)
+    pos_score = score_scale * jnp.sum(embq_ref[...].astype(f32) * positive, axis=1, keepdims=True)
+    pos_weight = jnp.exp(pos_score)
+
+    @pl.loop(1, 8)
+    def _(s):
+        q_copy(z, up(s)).wait_recv()
+
+    @pl.loop(1, 16)
+    def _(s):
+        fetch_copy(d, across(s)).wait_recv()
+
+    @pl.loop(1, 32)
+    def _(s):
+        index_copy(beyond(s), here).start()
+
+    own_index = pltpu.make_async_copy(slots.at[here], index_ref.at[here], idx_s.at[here])
+    own_index.start()
+
+    @pl.loop(0, 4)
+    def _(s):
+        pair = lax.rem(z // 2 + 1 + s, 4)
+        q = qall[pl.ds(pair * 2, 2)].reshape(64, 768)
+        cand = cands[pair].reshape(256, 768)
+        score = score_scale * lax.dot_general(
+            q, cand, (((1,), (1,)), ((), ())), preferred_element_type=f32)
+        row = lax.broadcasted_iota(jnp.int32, (64, 256), 0)
+        lane = lax.broadcasted_iota(jnp.int32, (64, 256), 1)
+        slot = ((lane >> 4) * 8 + z) * 8 + (lane & 7)
+        owned = column_ref[pl.ds(pl.multiple_of(pair * 64, 64), 64), :]
+        hit = (owned[:, 0:1] >> 8) == slot
+        for k in range(1, 8):
+            hit = hit | ((owned[:, k:k + 1] >> 8) == slot)
+        hit = hit & ((row >> 5) == ((lane >> 3) & 1))
+        weight = jnp.where(hit, jnp.exp(score), 0.0)
+        total = jnp.sum(weight, axis=1, keepdims=True)
+        summed = jnp.dot(weight.astype(bf16), cand, preferred_element_type=f32).astype(bf16)
+        high = total.astype(bf16)
+        low = (total - high.astype(f32)).astype(bf16)
+        first = lax.broadcasted_iota(jnp.int32, (64, 128), 1) < 64
+        tail = jnp.where(first, high.astype(f32), low.astype(f32)).astype(bf16)
+        for k in range(2):
+            m = pair * 2 + k
+            sums[m, :, 0:768] = summed[k * 32:(k + 1) * 32]
+            sums[m, :, 768:896] = tail[k * 32:(k + 1) * 32]
+
+            @pl.when(m != z)
+            def _():
+                sums_copy(m, z).start()
+
+    sums_in[z] = sums[z]
+
+    @pl.loop(1, 8)
+    def _(s):
+        sums_copy(z, up(s)).wait_recv()
+
+    gathered = sums_in[0].astype(f32)
+    for m in range(1, 8):
+        gathered = gathered + sums_in[m].astype(f32)
+    total = gathered[:, 768:769] + gathered[:, 832:833] + pos_weight
+    loss = jnp.log(total) - pos_score
+    diagonal = lax.broadcasted_iota(jnp.int32, (32, 32), 0) == lax.broadcasted_iota(jnp.int32, (32, 32), 1)
+    loss_ref[...] = jnp.sum(jnp.where(diagonal, loss, 0.0), axis=0, keepdims=True)
+    dunit = score_scale * ((gathered[:, 0:768] + pos_weight * positive) / total - positive)
+    along = jnp.sum(unit * dunit, axis=1, keepdims=True)
+    draw[...] = ((dunit - unit * along) / length).astype(bf16)
+
+    @pl.loop(1, 8)
+    def _(s):
+        draw_copy(up(s), z).start()
+
+    draws[z] = draw[...]
+
+    @pl.loop(1, 8)
+    def _(s):
+        piece_copy(z, up(s)).wait_recv()
+
+    @pl.loop(1, 8)
+    def _(s):
+        draw_copy(z, up(s)).wait_recv()
+
+    term = lax.dot_general(
+        pieces_in[...].reshape(256, 256), draws[...].reshape(256, 768), (((0,), (0,)), ((), ())),
+        preferred_element_type=f32)
+    upper = (lax.broadcasted_iota(jnp.int32, (256, 384), 0) & 7) < 4
+    gshare[...] = jnp.where(upper, term[:, 0:384], term[:, 384:768]).reshape(32, 8, 384)
+
+    @pl.loop(1, 32)
+    def _(s):
+        grad_copy(beyond(s), here).start()
+
+    gshare_in[here] = gshare[here]
+
+    @pl.loop(1, 32)
+    def _(s):
+        grad_copy(here, beyond(s)).wait_recv()
+
+    grad = jnp.sum(gshare_in[...], axis=0)
+    grad_ref[:, 0:384] = grad[0:4]
+    grad_ref[:, 384:768] = grad[4:8]
+
+    @pl.loop(1, 32)
+    def _(s):
+        index_copy(here, beyond(s)).wait_recv()
+
+    own_index.wait()
+
+    @pl.loop(1, 8)
+    def _(s):
+        q_copy(up(s), z).wait_send()
+        piece_copy(up(s), z).wait_send()
+        sums_copy(up(s), z).wait_send()
+        draw_copy(up(s), z).wait_send()
+
+    @pl.loop(1, 16)
+    def _(s):
+        fetch_copy(across(s), d).wait_send()
+
+    @pl.loop(1, 32)
+    def _(s):
+        index_copy(beyond(s), here).wait_send()
+        grad_copy(beyond(s), here).wait_send()
+
+
+def exchange(embc, embq, unitq, lenq, sumq, codes, column, idx, pos):
+    vmem = pl.BlockSpec(memory_space=pltpu.VMEM)
+    sds = jax.ShapeDtypeStruct
+    dma = pltpu.SemaphoreType.DMA
+    return pl.pallas_call(
+        exchange_kernel,
+        out_shape=(sds((1, 32), f32), sds((4, 768), f32), sds((32, 16, 768), bf16)),
+        in_specs=[vmem] * 9,
+        out_specs=[vmem, vmem, pl.BlockSpec(memory_space=pl.ANY)],
+        scratch_shapes=[
+            pltpu.VMEM((16, 4, 16, 768), bf16),
+            pltpu.VMEM((4, 16, 16, 768), bf16),
+            pltpu.VMEM((8, 32, 768), bf16),
+            pltpu.VMEM((256, 256), f32),
+            pltpu.VMEM((32, 16, 768), bf16),
+            pltpu.VMEM((8, 32, 256), bf16),
+            pltpu.VMEM((8, 32, 256), bf16),
+            pltpu.VMEM((8, 32, 896), bf16),
+            pltpu.VMEM((8, 32, 896), bf16),
+            pltpu.VMEM((32, 768), bf16),
+            pltpu.VMEM((8, 32, 768), bf16),
+            pltpu.VMEM((32, 8, 384), f32),
+            pltpu.VMEM((32, 8, 384), f32),
+            dma((16,)), dma((16,)), dma((8,)), dma((8,)), dma((8,)), dma((8,)), dma((32,)), dma((32,)),
+            dma((8,)), dma((8,)), dma((8,)), dma((8,)), dma((32,)), dma((32,)),
+        ],
+        compiler_params=pltpu.CompilerParams(
+            collective_id=1, has_side_effects=True, vmem_limit_bytes=48 * 1024 * 1024),
+        cost_estimate=pl.CostEstimate(flops=2_500_000_000, bytes_accessed=4_000_000, transcendentals=100_000),
+        name="exchange",
+    )(embc, embq, unitq, lenq, sumq, codes, column, idx, pos)
+
+
+def ranks_of(ids):
+    count = ids.shape[0]
+    earlier = jnp.arange(count)[None, :] < jnp.arange(count)[:, None]
+    return jnp.sum(((ids[:, None] == ids[None, :]) & earlier).astype(jnp.int32), axis=1)
 
 
 def per_device(
     queries, clips, norm_gain, w_in, w_out, proj, pos_row, neg_owner, neg_row, clip_dest
 ):
     width = queries.shape[1]
-    query_rows = pos_row.shape[0]
-    clip_rows = clip_dest.shape[0]
-    clip_embed, query_embed, query_unit, query_length, query_summed = encode(
+    asked = neg_owner.reshape(-1)
+    code = (asked * 8 + ranks_of(asked)) * 256 + neg_row.reshape(-1)
+    codes = lax.all_gather(code, ("dp", "mp"), axis=0, tiled=False)
+    destination = clip_dest[:, 0]
+    idx = (destination * 16 + ranks_of(destination)).reshape(1, -1)
+    embc, embq, unitq, lenq, sumq = encode(
         queries, clips, norm_gain.reshape(1, width), w_in.reshape(width, -1), w_out, proj)
-    query_length = query_length[:, :1]
-    embed_width = clip_embed.shape[1]
-    owners = lax.axis_size(("group", "dp"))
-    destination = clip_dest[:, 0]
-    cap_index = max(2, min(clip_rows, 2 * clip_rows // owners))
-    place_index = destination * cap_index + slots_of(destination, owners)
-    outgoing = (
-        jnp.zeros((owners * cap_index, embed_width), jnp.bfloat16).at[place_index].set(clip_embed)
-    )
-    received = lax.all_to_all(
-        outgoing.reshape(owners, cap_index, embed_width),
-        ("group", "dp"),
-        split_axis=0,
-        concat_axis=0,
-        tiled=True,
-    )
-    index_shard = received.reshape(owners * cap_index, embed_width)
-    peers = lax.axis_size(("dp", "mp"))
-    negatives = neg_owner.shape[1]
-    cap_fetch = max(2, min(query_rows, 4 * query_rows * negatives // peers))
-    flat_owner = neg_owner.reshape(-1)
-    place_fetch = flat_owner * cap_fetch + slots_of(flat_owner, peers)
-    wanted = jnp.zeros((peers * cap_fetch,), jnp.int32).at[place_fetch].set(neg_row.reshape(-1))
-    fetched = lax.all_to_all(
-        clip_embed[
-            lax.all_to_all(
-                wanted.reshape(peers, cap_fetch),
-                ("dp", "mp"),
-                split_axis=0,
-                concat_axis=0,
-                tiled=True,
-            )
-        ],
-        ("dp", "mp"),
-        split_axis=0,
-        concat_axis=0,
-        tiled=True,
-    )
-    negative_embed = fetched.reshape(peers * cap_fetch, embed_width)[place_fetch].reshape(
-        query_rows, negatives, embed_width
-    )
-    positive_embed = clip_embed[pos_row]
-    candidates = jnp.concatenate([positive_embed[:, None, :], negative_embed], axis=1).astype(
-        jnp.float32
-    )
-    scores = score_scale * jnp.einsum("qe,qce->qc", query_embed.astype(jnp.float32), candidates)
-    weights = jnp.exp(scores)
-    total = jnp.sum(weights, axis=-1)
-    losses = jnp.log(total) - scores[:, 0]
-    probs = weights / total[:, None]
-    dunit = score_scale * (jnp.einsum("qc,qce->qe", probs, candidates) - candidates[:, 0, :])
-    along = jnp.sum(query_unit * dunit, axis=-1, keepdims=True)
-    draw = ((dunit - query_unit * along) / query_length).astype(jnp.bfloat16)
-    slices = lax.axis_size("mp")
-    pieces = query_summed.reshape(query_rows, owners, slices, -1).transpose(2, 0, 1, 3)
-    pieces = lax.all_to_all(
-        pieces.reshape(slices, query_rows, -1), "mp", split_axis=0, concat_axis=0, tiled=True)
-    draws = lax.all_gather(draw, "mp", axis=0, tiled=True)
-    term = lax.dot_general(
-        pieces.reshape(slices * query_rows, -1), draws, (((0,), (0,)), ((), ())),
-        preferred_element_type=jnp.float32)
-    shares = lax.all_to_all(
-        term.reshape(owners, -1, embed_width), ("group", "dp"), split_axis=0, concat_axis=0, tiled=True)
-    grad_proj = jnp.sum(shares, axis=0)
-    return (losses, index_shard, grad_proj)
+    column = lax.dynamic_slice_in_dim(codes, lax.axis_index("dp") * 8, 8, 0).reshape(256, 8)
+    loss, grad, index = exchange(
+        embc, embq, unitq, lenq, sumq, codes, column, idx, pos_row.reshape(-1, 1))
+    return (loss.reshape(-1), index.reshape(-1, index.shape[-1]), grad)
 
 
 def solution(mesh):

time: 189 us -> 457 us (2.42)
  blocking collectives: 20 us -> 288 us
  Pallas kernels: 43.3 us -> 163 us
  starting transfers between devices: 53.3 us -> 0 us
  waiting for transfers between devices: 46.2 us -> 0 us
  local copies, waits for them, and re-layouts: 19.9 us -> 5.13 us
    all_gather x1, blocking collectives: 20 us -> 288 us  [per_device(): codes = lax.all_gather(code, ('dp', 'mp'), axis=0, tiled=False)]
    pallas_call x0 -> x1, Pallas kernels: none -> 115 us  [exchange(): pl.pallas_call(exchange_kernel, out_shape=(sds((1, 32), f32), sds((4, 768...]
    all_to_all x5 -> x0, starting transfers between devices: 53.3 us -> none  [the longest x1 16.3 us: per_device(): lax.all_to_all(wanted.reshape(peers, cap_fetch), ('dp', 'mp'), split_axis...]
    all_to_all x5 -> x0, waiting for transfers between devices: 46.2 us -> none  [the longest x1 35.3 us: per_device(): lax.all_to_all(clip_embed[lax.all_to_all(wanted.reshape(peers, cap_fetch)...]
    gather x3 -> x0, local copies, waits for them, and re-layouts: 7.03 us -> none  [the longest x1 5.21 us: per_device(): clip_embed[lax.all_to_all(wanted.reshape(peers, cap_fetch), ('dp', 'mp'),...]
    pallas_call x1, Pallas kernels: 43.3 us -> 48.2 us  [encode(): pl.pallas_call(encode_kernel, out_shape=(sds((256, 768), bf16), sds((32,...]
  transfers between devices with their start and end apart: 5 -> 0, of which waited for: 3 -> 0; matrix products, arithmetic and copies ran while one was open for 9% -> 0% of each run, Pallas kernels for 23% -> 0%
where the time goes in v2:
time: 457 us
  blocking collectives  288 us (63%)
  Pallas kernels  163 us (36%)
  local copies, waits for them, and re-layouts  5.13 us (1%)
    all_gather x1, blocking collectives, per_device(): codes = lax.all_gather(code, ('dp', 'mp'), axis=0, tiled=False)  288 us
    pallas_call x1, Pallas kernels, exchange(): pl.pallas_call(exchange_kernel, out_shape=(sds((1, 32), f32), sds((4, 768...  115 us
    pallas_call x1, Pallas kernels, encode(): pl.pallas_call(encode_kernel, out_shape=(sds((256, 768), bf16), sds((32,...  48.2 us

profile of v2, /device:TPU:1, one launch (start us, length us, event | category | flops | bytes accessed | tf_op | source)
XLA Modules:
  0.0 457.2 jit_solution(1335553454615837136)
XLA Ops:
  0.6 0.0 copy-start
  0.6 0.0 copy-start.1
  0.7 0.0 copy-start.2
  0.7 0.0 copy-start.3
  0.7 2.3 copy.27
  3.0 0.0 copy-done
  3.0 0.0 copy-done.1
  3.0 0.1 copy-done.2
  3.1 0.0 copy-done.3
  3.1 0.0 copy-start.6
  3.1 0.0 copy-start.4
  3.1 0.0 copy-start.5
  3.1 0.0 copy-start.7
  3.1 48.2 %encode.1 = (bf16[256,768]{1,0:T(8,128)(2,1)S(1)}, bf16[32,768]{1,0:T(8,128)(2,1)S(1)}, f32[32,768]{1,0:T(8,128)S(1)}, f32[32,128]{1,0:T(8,128)S(1)}, bf16[32,1024]{1,0:T(8,128)(2,1)S(1)}) custom-call(bf16[256,1024]{1,0:T(8,128)(2,1)S(1)} %copy-done.2, bf16[2048,1024]{1,0:T(8,128)(2,1)} %c_hbm.1, f32[1,1024]{1,0:T(1,128)S(1)} %bitcast.19, ...), custom_call_target="tpu_custom_call" | custom-call | flops 8499999744 | bytes 20000000 | tf_op jit(solution)/shard_map/encode/pallas_call | solution.py:178
  51.3 0.0 copy-done.6
  51.3 0.1 copy.24
  51.4 0.1 reshape.85
  51.5 0.0 copy-done.4
  51.5 0.1 copy.22
  51.6 0.1 mul.50
  51.7 0.1 copy.23
  51.7 0.1 eq.30
  51.8 0.2 convert_reduce_fusion.1
  52.0 288.1 %all-gather = s32[128,1,256]{2,1,0:T(1,128)S(1)} all-gather(s32[1,1,256]{2,1,0:T(1,128)S(1)} %add_bitcast_fusion), channel_id=1, replica_groups=mesh['group'=2,'dp'=16,'mp'=8] {'dp','mp'}, dimensions={0}, use_global_device_ids=true | all-gather | bytes 132096 | tf_op jit(solution)/shard_map/all_gather | solution.py:505
  340.1 0.1 reshape.86.column_ref
  340.2 0.0 copy-done.5
  340.3 0.2 convert_reduce_fusion
  340.4 0.0 copy-done.7
  340.5 0.1 copy.25.pos_ref
  340.5 114.7 %exchange.1 = (f32[1,32]{1,0:T(1,128)S(1)}, f32[4,768]{1,0:T(4,128)S(1)}, bf16[32,16,768]{2,1,0:T(8,128)(2,1)S(1)}) custom-call(bf16[256,768]{1,0:T(8,128)(2,1)S(1)} %get-tuple-element.11.embc_ref, bf16[32,768]{1,0:T(8,128)(2,1)S(1)} %get-tuple-element.12.embq_ref, f32[32,768]{1,0:T(8,128)S(1)} %get-tuple-element.13.unitq_ref, ...), custom_call_target="tpu_custom_call" | custom-call | flops 2500000000 | bytes 4000000 | tf_op jit(solution)/shard_map/exchange/pallas_call | solution.py:464
  455.2 0.5 copy.33
  455.7 0.9 copy.34
  456.6 0.6 copy.35
  (5 shorter events, 0.1 us)
Async XLA Ops:
  0.6 2.4 copy-start
  0.6 2.4 copy-start.1
  0.7 2.4 copy-start.2
  0.7 2.4 copy-start.3
  3.1 48.2 %copy-start.6 = (s32[32,8]{0,1:T(8,128)S(1)}, s32[32,8]{0,1:T(8,128)}, u32[]{:S(2)}) copy-start(s32[32,8]{0,1:T(8,128)} %param.18) | copy-start | bytes 3076
  3.1 48.4 %copy-start.4 = (s32[32,8]{0,1:T(8,128)S(1)}, s32[32,8]{0,1:T(8,128)}, u32[]{:S(2)}) copy-start(s32[32,8]{0,1:T(8,128)} %param.17) | copy-start | bytes 3076
  3.1 337.1 %copy-start.5 = (s32[256,1]{0,1:T(1,128)S(1)}, s32[256,1]{0,1:T(1,128)}, u32[]{:S(2)}) copy-start(s32[256,1]{0,1:T(1,128)} %param.19) | copy-start | bytes 3076
  3.1 337.3 %copy-start.7 = (s32[32]{0:T(128)S(1)}, s32[32]{0:T(128)}, u32[]{:S(2)}) copy-start(s32[32]{0:T(128)} %param.16) | copy-start | bytes 388

commit v3 on v0

v3 whole, which is shorter than its diff:
```python
import jax
import jax.numpy as jnp
from jax import lax
from jax.experimental import pallas as pl
from jax.experimental.pallas import tpu as pltpu
from jax.sharding import PartitionSpec as P

norm_eps = 1e-06
embed_eps = 1e-06
score_scale = 20.0
MESH = pl.DeviceIdType.MESH
f32 = jnp.float32
bf16 = jnp.bfloat16
FAR_FIRST = (
    (2, 2), (3, 2), (2, 3), (2, 1), (1, 2), (3, 1), (1, 3), (3, 3), (1, 1), (0, 2), (2, 0), (3, 0), (0, 3), (1, 0),
    (0, 1),
)


def part_of(way, dist):
    return 0 if dist == 4 else 8 - 2 * dist + way


def kernel(
    q_hbm, c_hbm, gain_ref, win_hbm, wout_hbm, proj_hbm, code_ref, mine_ref, idx_ref, pos_ref,
    loss_ref, grad_ref, index_ref,
    x, win, wout, proj, woutp, normed, hidden, cpart, qpart, base, crecv, qrecv,
    codes, column, onehots, packed, embc, embq, sumq,
    fetch, cands, qall, slots, pieces, pieces_in, sums, sums_in, draw, draws, gshare, gshare_in,
    load_sem, c_s, c_r, qp_s, qp_r, code_s, code_r, col_s, col_r, plane_s, plane_r,
    fetch_s, fetch_r, q_s, q_r, piece_s, piece_r, idx_s, idx_r, sums_s, sums_r, draw_s, draw_r, grad_s, grad_r,
):
    g, d, z = lax.axis_index("group"), lax.axis_index("dp"), lax.axis_index("mp")
    y, xx = d // 4, lax.rem(d, 4)
    here = g * 16 + d
    right, left = lax.rem(z + 1, 8), lax.rem(z + 7, 8)

    def up(s):
        return lax.rem(z + s, 8)

    def across(dy, dx):
        return lax.rem(y + dy, 4) * 4 + lax.rem(xx + dx, 4)

    def owner(o):
        return {"group": o // 16, "dp": lax.rem(o, 16)}

    def remote(src, dst, send, recv, target):
        return pltpu.make_async_remote_copy(
            src_ref=src, dst_ref=dst, send_sem=send, recv_sem=recv, device_id=target, device_id_type=MESH)

    def home_of(i):
        even = (8 - i) // 2
        odd = 8 - (9 - i) // 2
        return lax.rem(z + jnp.where(lax.rem(i, 2) == 0, even, odd), 8)

    def load_x(i):
        rows = pl.ds(pl.multiple_of(home_of(jnp.int32(i)) * 256, 256), 256)
        return pltpu.make_async_copy(c_hbm.at[rows], x.at[i], load_sem.at[i])

    load_q = pltpu.make_async_copy(q_hbm, x.at[1], load_sem.at[1])
    load_in = pltpu.make_async_copy(win_hbm, win, load_sem.at[9])
    load_out = pltpu.make_async_copy(wout_hbm, wout, load_sem.at[10])
    load_proj = pltpu.make_async_copy(proj_hbm, proj, load_sem.at[11])
    load_x(0).start()
    load_out.start()
    load_proj.start()
    load_in.start()
    load_q.start()
    for i in range(2, 9):
        load_x(i).start()

    barrier = pltpu.get_barrier_semaphore()

    @pl.loop(1, 32)
    def _(s):
        pl.semaphore_signal(barrier, inc=1, device_id=owner(lax.rem(here + s, 32)), device_id_type=MESH)

    @pl.loop(1, 8)
    def _(s):
        pl.semaphore_signal(barrier, inc=1, device_id={"mp": up(s)}, device_id_type=MESH)

    def code_copy(to, frm):
        return remote(code_ref.at[0], codes.at[d, frm], code_s.at[to], code_r.at[frm], {"mp": to})

    def column_copy(to, frm):
        return remote(mine_ref, column.at[frm], col_s.at[to], col_r.at[frm], {"mp": to})

    def plane_copy(to, frm):
        return remote(codes.at[frm], codes.at[frm], plane_s.at[to], plane_r.at[frm], {"dp": to})

    def q_copy(to, frm):
        return remote(embq, qall.at[frm], q_s.at[to], q_r.at[frm], {"mp": to})

    def fetch_copy(pair, to, frm):
        return remote(
            fetch.at[pair, to], cands.at[pair, frm], fetch_s.at[pair, to], fetch_r.at[pair, frm], {"dp": to})

    def piece_copy(to, frm):
        return remote(pieces.at[to // 2], pieces_in.at[frm], piece_s.at[to], piece_r.at[frm], {"mp": to})

    def index_copy(to, frm):
        return remote(slots.at[to], index_ref.at[frm], idx_s.at[to], idx_r.at[frm], owner(to))

    def sums_copy(to, frm):
        return remote(sums.at[to], sums_in.at[frm], sums_s.at[to], sums_r.at[frm], {"mp": to})

    def draw_copy(to, frm):
        return remote(draw, draws.at[frm], draw_s.at[to], draw_r.at[frm], {"mp": to})

    def grad_copy(to, frm):
        return remote(gshare.at[to], gshare_in.at[frm], grad_s.at[to], grad_r.at[frm], owner(to))

    def spot(way, u):
        if u == 0:
            dist, half = 4, way
        elif u % 2 == 1:
            dist, half = 4 - (u + 1) // 2, 1 - way
        else:
            dist, half = 4 - u // 2, way
        return part_of(way, dist), slice(half * 128, half * 128 + 128), slice(half * 16, half * 16 + 16)

    def c_copy(way, u):
        i, rows, _ = spot(way, u)
        return remote(
            cpart.at[i, rows], crecv.at[way, u], c_s.at[way, u], c_r.at[way, u],
            {"mp": right if way == 0 else left})

    def qp_copy(way, u):
        i, _, rows = spot(way, u)
        return remote(
            qpart.at[i, rows], qrecv.at[way, u], qp_s.at[way, u], qp_r.at[way, u],
            {"mp": right if way == 0 else left})

    def q_unit(way, u):
        i, _, rows = spot(way, u)
        if u >= 2:
            qp_copy(way, u - 2).wait_recv()
            qpart[i, rows] = (qpart[i, rows].astype(f32) + qrecv[way, u - 2].astype(f32)).astype(bf16)
        qp_copy(way, u).start()

    def c_unit(way, u):
        i, rows, _ = spot(way, u)
        if u >= 2:
            c_copy(way, u - 2).wait_recv()
            cpart[i, rows] = (cpart[i, rows].astype(f32) + crecv[way, u - 2].astype(f32)).astype(bf16)
        c_copy(way, u).start()

    def both_units(u):
        q_unit(0, u)
        q_unit(1, u)
        c_unit(0, u)
        c_unit(1, u)

    load_out.wait()
    load_proj.wait()
    woutp[...] = jnp.dot(wout[...], proj[...], preferred_element_type=f32).astype(bf16)

    @pl.loop(0, 9)
    def _(i):
        @pl.when(i == 1)
        def _():
            load_q.wait()

        @pl.when(i != 1)
        def _():
            load_x(i).wait()

        @pl.loop(0, 8)
        def _(r):
            rows = pl.ds(pl.multiple_of(r * 32, 32), 32)
            v = x[i, rows, :].astype(f32)
            scale = lax.rsqrt(jnp.mean(v * v, axis=-1, keepdims=True) + norm_eps)
            normed[rows, :] = (v * scale * gain_ref[...]).astype(bf16)

        @pl.when(i == 0)
        def _():
            load_in.wait()

        for n in range(2):
            gate = jnp.dot(normed[...], win[:, n * 256:(n + 1) * 256], preferred_element_type=f32)
            upper = jnp.dot(normed[...], win[:, 512 + n * 256:768 + n * 256], preferred_element_type=f32)
            hidden[:, n * 256:(n + 1) * 256] = (gate / (1.0 + jnp.exp(-gate)) * upper).astype(bf16)

        @pl.when(i == 0)
        def _():
            pl.semaphore_wait(barrier, 38)

        @pl.when(i == 1)
        def _():
            normed[...] = jnp.dot(hidden[...], wout[...], preferred_element_type=f32).astype(bf16)
            for k in (0, 2, 3, 4, 5, 6, 7, 8):
                h = home_of(jnp.int32(k))
                qpart[k] = normed[pl.ds(pl.multiple_of(h * 32, 32), 32), :]
            q_unit(0, 0)
            q_unit(1, 0)

        @pl.when(i != 1)
        def _():
            cpart[i] = jnp.dot(hidden[...], woutp[...], preferred_element_type=f32).astype(bf16)

        @pl.when(i == 0)
        def _():
            c_unit(0, 0)
            c_unit(1, 0)

            @pl.loop(1, 8)
            def _(s):
                code_copy(up(s), z).start()
                column_copy(up(s), z).start()

            codes[d, z] = code_ref[0]
            column[z] = mine_ref[...]

        @pl.when(i == 2)
        def _():
            q_unit(0, 1)
            c_unit(0, 1)

        @pl.when(i == 3)
        def _():
            q_unit(1, 1)
            c_unit(1, 1)

        @pl.when(i == 5)
        def _():
            both_units(2)

        @pl.when(i == 6)
        def _():
            @pl.loop(1, 8)
            def _(s):
                code_copy(z, up(s)).wait_recv()
                column_copy(z, up(s)).wait_recv()

            @pl.loop(1, 16)
            def _(s):
                plane_copy(lax.rem(d + s, 16), d).start()

    both_units(3)
    base[...] = jnp.dot(x[8], proj[...], preferred_element_type=f32) + cpart[8].astype(f32)

    @pl.loop(1, 16)
    def _(s):
        plane_copy(d, lax.rem(d + s, 16)).wait_recv()

    owner_slot = (d * 8 + z) * 8

    def wanted(pair):
        rank = lax.broadcasted_iota(jnp.int32, (8, 256), 0)
        lane = lax.broadcasted_iota(jnp.int32, (8, 256), 1)
        for c in range(16):
            for k in range(2):
                code = codes[c, pair * 2 + k]
                hit = (code >> 8) == owner_slot + rank
                row = jnp.sum(jnp.where(hit, (code & 255) + 1, 0), axis=1, keepdims=True) - 1
                packed[c * 16 + k * 8:c * 16 + k * 8 + 8, :] = jnp.where(lane == row, 1.0, 0.0)
        onehots[pair] = packed[...].astype(bf16)

    @pl.loop(0, 2)
    def _(pair):
        wanted(pair)

    both_units(4)

    @pl.loop(2, 4)
    def _(pair):
        wanted(pair)

    both_units(5)
    both_units(6)

    for way in (0, 1):
        for u in (5, 6):
            qp_copy(way, u).wait_recv()
    for half in range(2):
        rows = slice(half * 16, half * 16 + 16)
        own = x[1, pl.ds(pl.multiple_of(z * 32 + half * 16, 16), 16), :].astype(f32)
        mixed = (
            qpart[8, rows].astype(f32) + qrecv[0, 6 - half].astype(f32) + qrecv[1, 5 + half].astype(f32))
        sumq[rows, :] = (own + mixed).astype(bf16)
    raw = jnp.dot(sumq[...], proj[...], preferred_element_type=f32)
    length = jnp.sqrt(jnp.sum(raw * raw, axis=-1, keepdims=True) + embed_eps)
    unit = raw / length
    embq[...] = unit.astype(bf16)
    qall[z] = embq[...]
    for s in (6, 7, 5, 4, 3, 2, 1):
        q_copy(up(s), z).start()

    for way in (0, 1):
        for u in (5, 6):
            c_copy(way, u).wait_recv()
    for half in range(2):
        for r in range(0, 128, 64):
            rows = slice(half * 128 + r, half * 128 + r + 64)
            raw_c = (
                base[rows, :] + crecv[0, 6 - half, r:r + 64].astype(f32)
                + crecv[1, 5 + half, r:r + 64].astype(f32))
            inverse = lax.rsqrt(jnp.sum(raw_c * raw_c, axis=-1, keepdims=True) + embed_eps)
            embc[rows, :] = (raw_c * inverse).astype(bf16)

    def pair_at(s):
        return lax.rem(z // 2 + 1 + s, 4)

    @pl.loop(0, 4)
    def _(s):
        pair = pair_at(s)
        rows = jnp.dot(onehots[pair], embc[...], preferred_element_type=f32).astype(bf16)
        fetch[pair] = rows.reshape(16, 16, 768)
        for dy, dx in FAR_FIRST:
            fetch_copy(pair, across(dy, dx), d).start()
        cands[pair, d] = fetch[pair, d]

    turned = sumq[...].astype(f32).T.reshape(32, 4, 8, 32)
    for k in range(4):
        pieces[k] = turned[:, k].reshape(256, 32).T.astype(bf16)

    @pl.loop(1, 8)
    def _(s):
        piece_copy(up(s), z).start()

    pieces_in[z] = pieces[z // 2]

    @pl.loop(0, 2)
    def _(s):
        row = lax.broadcasted_iota(jnp.int32, (256, 256), 0) + s * 256
        onehot = jnp.where(row == idx_ref[...], 1.0, 0.0).astype(bf16)
        rows = jnp.dot(onehot, embc[...], preferred_element_type=f32).astype(bf16)
        slots[pl.ds(s * 16, 16)] = rows.reshape(16, 16, 768)

    at_pos = lax.broadcasted_iota(jnp.int32, (32, 256), 1) == pos_ref[...]
    positive = jnp.dot(jnp.where(at_pos, 1.0, 0.0).astype(bf16), embc[...], preferred_element_type=f32)
    pos_score = score_scale * jnp.sum(embq[...].astype(f32) * positive, axis=1, keepdims=True)
    pos_weight = jnp.exp(pos_score)

    @pl.loop(0, 4)
    def _(s):
        pair = pair_at(s)
        for k in range(2):
            @pl.when(pair * 2 + k != z)
            def _():
                q_copy(z, pair * 2 + k).wait_recv()

        @pl.loop(1, 16)
        def _(t):
            fetch_copy(pair, d, lax.rem(d + t, 16)).wait_recv()

        q = qall[pl.ds(pair * 2, 2)].reshape(64, 768)
        cand = cands[pair].reshape(256, 768)
        score = score_scale * lax.dot_general(
            q, cand, (((1,), (1,)), ((), ())), preferred_element_type=f32)
        row = lax.broadcasted_iota(jnp.int32, (64, 256), 0)
        lane = lax.broadcasted_iota(jnp.int32, (64, 256), 1)
        slot = ((lane >> 4) * 8 + z) * 8 + (lane & 7)
        asked = column[pl.ds(pair * 2, 2)].reshape(64, 8)
        hit = (asked[:, 0:1] >> 8) == slot
        for k in range(1, 8):
            hit = hit | ((asked[:, k:k + 1] >> 8) == slot)
        hit = hit & ((row >> 5) == ((lane >> 3) & 1))
        weight = jnp.where(hit, jnp.exp(score), 0.0)
        total = jnp.sum(weight, axis=1, keepdims=True)
        summed = jnp.dot(weight.astype(bf16), cand, preferred_element_type=f32).astype(bf16)
        high = total.astype(bf16).astype(f32)
        first = lax.broadcasted_iota(jnp.int32, (64, 128), 1) < 64
        tail = jnp.where(first, high, total - high).astype(bf16)
        for k in range(2):
            sums[pair * 2 + k, :, 0:768] = summed[k * 32:(k + 1) * 32]
            sums[pair * 2 + k, :, 768:896] = tail[k * 32:(k + 1) * 32]

            @pl.when(pair * 2 + k != z)
            def _():
                sums_copy(pair * 2 + k, z).start()

    sums_in[z] = sums[z]
    own_index = pltpu.make_async_copy(slots.at[here], index_ref.at[here], idx_s.at[here])
    own_index.start()
    for dy, dx in FAR_FIRST:
        for k in range(2):
            index_copy(k * 16 + across(dy, dx), here).start()
    index_copy((1 - g) * 16 + d, here).start()

    @pl.loop(1, 8)
    def _(s):
        sums_copy(z, up(s)).wait_recv()

    gathered = sums_in[0].astype(f32)
    for m in range(1, 8):
        gathered = gathered + sums_in[m].astype(f32)
    total = gathered[:, 768:769] + gathered[:, 832:833] + pos_weight
    loss = jnp.log(total) - pos_score
    diagonal = lax.broadcasted_iota(jnp.int32, (32, 32), 0) == lax.broadcasted_iota(jnp.int32, (32, 32), 1)
    loss_ref[...] = jnp.sum(jnp.where(diagonal, loss, 0.0), axis=0, keepdims=True)
    dunit = score_scale * ((gathered[:, 0:768] + pos_weight * positive) / total - positive)
    along = jnp.sum(unit * dunit, axis=1, keepdims=True)
    draw[...] = ((dunit - unit * along) / length).astype(bf16)
    for s in (4, 3, 5, 2, 6, 1, 7):
        draw_copy(up(s), z).start()
    draws[z] = draw[...]

    @pl.loop(1, 8)
    def _(s):
        piece_copy(z, up(s)).wait_recv()

    @pl.loop(1, 8)
    def _(s):
        draw_copy(z, up(s)).wait_recv()

    term = lax.dot_general(
        pieces_in[...].reshape(256, 256), draws[...].reshape(256, 768), (((0,), (0,)), ((), ())),
        preferred_element_type=f32).reshape(32, 8, 768)
    turned_term = jnp.concatenate([term[:, 4:8], term[:, 0:4]], axis=1)
    even = lax.rem(z, 2) == 0
    upper_rows = lax.broadcasted_iota(jnp.int32, (32, 8, 384), 1) < 4
    gshare[...] = jnp.where(
        upper_rows,
        jnp.where(even, term[:, :, 0:384], turned_term[:, :, 0:384]),
        jnp.where(even, turned_term[:, :, 384:768], term[:, :, 384:768]))
    for dy, dx in FAR_FIRST:
        for k in range(2):
            grad_copy(k * 16 + across(dy, dx), here).start()
    grad_copy((1 - g) * 16 + d, here).start()
    gshare_in[here] = gshare[here]

    for way in (0, 1):
        for u in range(7):
            qp_copy(way, u).wait_send()
            c_copy(way, u).wait_send()

    @pl.loop(1, 8)
    def _(s):
        code_copy(up(s), z).wait_send()
        column_copy(up(s), z).wait_send()
        q_copy(up(s), z).wait_send()
        piece_copy(up(s), z).wait_send()
        sums_copy(up(s), z).wait_send()
        draw_copy(up(s), z).wait_send()

    @pl.loop(1, 16)
    def _(s):
        to = lax.rem(d + s, 16)
        plane_copy(to, d).wait_send()
        for pair in range(4):
            fetch_copy(pair, to, d).wait_send()

    own_index.wait()

    @pl.loop(1, 32)
    def _(s):
        other = lax.rem(here + s, 32)
        index_copy(other, here).wait_send()
        index_copy(here, other).wait_recv()

    @pl.loop(1, 32)
    def _(s):
        other = lax.rem(here + s, 32)
        grad_copy(other, here).wait_send()
        grad_copy(here, other).wait_recv()

    grad = jnp.sum(gshare_in[...], axis=0)
    grad_ref[:, 0:384] = grad[0:4]
    grad_ref[:, 384:768] = grad[4:8]


def fused(queries, clips, gain, win, wout, proj, code, mine, idx, pos):
    hbm = pl.BlockSpec(memory_space=pl.ANY)
    vmem = pl.BlockSpec(memory_space=pltpu.VMEM)
    sds = jax.ShapeDtypeStruct
    dma = pltpu.SemaphoreType.DMA
    return pl.pallas_call(
        kernel,
        out_shape=(sds((1, 32), f32), sds((4, 768), f32), sds((32, 16, 768), bf16)),
        in_specs=[hbm, hbm, vmem, hbm, hbm, hbm, vmem, vmem, vmem, vmem],
        out_specs=[vmem, vmem, hbm],
        scratch_shapes=[
            pltpu.VMEM((9, 256, 1024), bf16),
            pltpu.VMEM((1024, 1024), bf16),
            pltpu.VMEM((512, 1024), bf16),
            pltpu.VMEM((1024, 768), bf16),
            pltpu.VMEM((512, 768), bf16),
            pltpu.VMEM((256, 1024), bf16),
            pltpu.VMEM((256, 512), bf16),
            pltpu.VMEM((9, 256, 768), bf16),
            pltpu.VMEM((9, 32, 1024), bf16),
            pltpu.VMEM((256, 768), f32),
            pltpu.VMEM((2, 7, 128, 768), bf16),
            pltpu.VMEM((2, 7, 16, 1024), bf16),
            pltpu.VMEM((16, 8, 1, 256), jnp.int32),
            pltpu.VMEM((8, 32, 8), jnp.int32),
            pltpu.VMEM((4, 256, 256), bf16),
            pltpu.VMEM((256, 256), f32),
            pltpu.VMEM((256, 768), bf16),
            pltpu.VMEM((32, 768), bf16),
            pltpu.VMEM((32, 1024), bf16),
            pltpu.VMEM((4, 16, 16, 768), bf16),
            pltpu.VMEM((4, 16, 16, 768), bf16),
            pltpu.VMEM((8, 32, 768), bf16),
            pltpu.VMEM((32, 16, 768), bf16),
            pltpu.VMEM((4, 32, 256), bf16),
            pltpu.VMEM((8, 32, 256), bf16),
            pltpu.VMEM((8, 32, 896), bf16),
            pltpu.VMEM((8, 32, 896), bf16),
            pltpu.VMEM((32, 768), bf16),
            pltpu.VMEM((8, 32, 768), bf16),
            pltpu.VMEM((32, 8, 384), f32),
            pltpu.VMEM((32, 8, 384), f32),
            dma((12,)), dma((2, 7)), dma((2, 7)), dma((2, 7)), dma((2, 7)), dma((8,)), dma((8,)), dma((8,)), dma((8,)),
            dma((16,)), dma((16,)), dma((4, 16)), dma((4, 16)), dma((8,)), dma((8,)), dma((8,)), dma((8,)),
            dma((32,)), dma((32,)), dma((8,)), dma((8,)), dma((8,)), dma((8,)), dma((32,)), dma((32,)),
        ],
        compiler_params=pltpu.CompilerParams(
            collective_id=0, has_side_effects=True, vmem_limit_bytes=52 * 1024 * 1024),
        cost_estimate=pl.CostEstimate(flops=11_000_000_000, bytes_accessed=20_000_000, transcendentals=2_000_000),
        name="fused",
    )(queries, clips, gain, win, wout, proj, code, mine, idx, pos)


def ranks_of(ids):
    count = ids.shape[0]
    earlier = jnp.arange(count)[None, :] < jnp.arange(count)[:, None]
    return jnp.sum(((ids[:, None] == ids[None, :]) & earlier).astype(jnp.int32), axis=1)


def per_device(
    queries, clips, norm_gain, w_in, w_out, proj, pos_row, neg_owner, neg_row, clip_dest
):
    width = queries.shape[1]
    asked = neg_owner.reshape(-1)
    code = (asked * 8 + ranks_of(asked)) * 256 + neg_row.reshape(-1)
    destination = clip_dest[:, 0]
    idx = destination * 16 + ranks_of(destination)
    loss, grad, index = fused(
        queries, clips, norm_gain.reshape(1, width), w_in.reshape(width, -1), w_out, proj,
        code.reshape(1, 1, -1), code.reshape(neg_owner.shape), idx.reshape(1, -1), pos_row.reshape(-1, 1))
    return (loss.reshape(-1), index.reshape(-1, index.shape[-1]), grad)


def solution(mesh):
    return jax.shard_map(
        per_device,
        mesh=mesh,
        in_specs=(
            P(("group", "dp"), None),
            P(("group", "dp"), None),
            P(),
            P(None, None, "mp"),
            P("mp", None),
            P(),
            P(("group", "dp", "mp")),
            P(("group", "dp", "mp"), None),
            P(("group", "dp", "mp"), None),
            P(("group", "dp", "mp"), None),
        ),
        out_specs=(
            P(("group", "dp", "mp")),
            P(("group", "dp", "mp"), None),
            P(("group", "dp", "mp"), None),
        ),
        check_vma=False,
    )
```

time: 477 us -> 108 us (0.23)
  waiting for transfers between devices: 369 us -> 0 us
  Pallas kernels: 0 us -> 96.6 us
  starting transfers between devices: 33.9 us -> 0 us
  other arithmetic: 20 us -> 1.83 us
  matrix products: 17 us -> 0 us
  between operations: 14.4 us -> 0.66 us
  local copies, waits for them, and re-layouts: 21.9 us -> 8.18 us
    unnamed x3 -> x0, waiting for transfers between devices: 236 us -> none
    pallas_call x0 -> x1, Pallas kernels: none -> 96.6 us  [fused(): pl.pallas_call(kernel, out_shape=(sds((1, 32), f32), sds((4, 768), f32),...]
    reduce_scatter x1 -> x0, waiting for transfers between devices: 78.8 us -> none  [per_device(): lax.psum_scatter(jnp.dot(hidden, w_out, preferred_element_type=jnp.float3...]
    all_to_all x3 -> x0, waiting for transfers between devices: 53.7 us -> none  [the longest x1 35.5 us: per_device(): lax.all_to_all(clip_embed[lax.all_to_all(wanted.reshape(peers, cap_fetch)...]
    all_to_all x3 -> x0, starting transfers between devices: 33.8 us -> none  [the longest x1 16.5 us: per_device(): lax.all_to_all(wanted.reshape(peers, cap_fetch), ('dp', 'mp'), split_axis...]
    dot_general x6 -> x0, matrix products: 17 us -> none  [the longest x1 5.11 us: per_device(): both = jnp.dot(normed, merged, preferred_element_type=jnp.float32)]
    convert_element_type x5 -> x0, other arithmetic: 11.7 us -> none  [the longest x1 7.04 us: per_device(): values = stacked.astype(jnp.float32)]
    gather x3 -> x0, local copies, waits for them, and re-layouts: 8.38 us -> none  [the longest x1 5.21 us: per_device(): clip_embed[lax.all_to_all(wanted.reshape(peers, cap_fetch), ('dp', 'mp'),...]
  transfers between devices with their start and end apart: 5 -> 0, of which waited for: 5 -> 0; matrix products, arithmetic and copies ran while one was open for 4% -> 0% of each run, Pallas kernels for 0% -> 0%
where the time goes in v3:
time: 108 us; the launch traced here: 107 us
  Pallas kernels  96.6 us (89%)
  local copies, waits for them, and re-layouts  8.18 us (8%)
  other arithmetic  1.83 us (2%)
    pallas_call x1, Pallas kernels, fused(): pl.pallas_call(kernel, out_shape=(sds((1, 32), f32), sds((4, 768), f32),...  96.6 us
    unnamed x10, local copies, waits for them, and re-layouts  7.1 us

profile of v3, /device:TPU:1, one launch (start us, length us, event | category | flops | bytes accessed | tf_op | source)
XLA Modules:
  0.0 107.3 jit_solution(2306774976588753499)
XLA Ops:
  0.6 0.9 convert_reduce_fusion
  1.6 0.7 bitcast_add_fusion.idx_ref
  2.3 0.8 copy.22
  3.0 0.1 eq.30
  3.1 0.2 convert_reduce_fusion.1
  3.3 0.8 copy.24
  4.1 0.1 reshape.85
  4.1 0.1 reduce_sum.26
  4.2 0.1 mul.53
  4.3 0.7 copy.26.pos_ref
  5.1 0.0 copy-start
  5.1 0.0 copy-start.1
  5.1 3.6 %copy.27 = bf16[128,8,2,512]{3,1,2,0:T(8,128)(2,1)} copy(bf16[128,8,2,512]{3,2,1,0:T(2,128)(2,1)} %bitcast.14) | data formatting | bytes 4194304
  8.7 0.0 copy-done
  8.7 0.0 copy-done.1
  8.7 96.6 %fused.1 = (f32[1,32]{1,0:T(1,128)S(1)}, f32[4,768]{1,0:T(4,128)S(1)}, bf16[32,16,768]{2,1,0:T(8,128)(2,1)S(1)}) custom-call(bf16[256,1024]{1,0:T(8,128)(2,1)S(1)} %copy-done, bf16[2048,1024]{1,0:T(8,128)(2,1)} %c_hbm.1, f32[1,1024]{1,0:T(1,128)S(1)} %bitcast.12, bf16[1024,1024]{1,0:T(8,128)(2,1)} %bitcast.15, bf16[512,1024]{1,0:T(8,128)(2,1)} %wout_hbm.1, ...), custom_call_target="tpu_custom_call" | custom-call | flops 11000000512 | bytes 20000000 | tf_op jit(solution)/shard_map/fused/pallas_call | solution.py:468
  105.3 0.5 copy.31
  105.8 0.9 copy.32
  106.7 0.6 copy.33
  (2 shorter events, 0.0 us)
Async XLA Ops:
  5.1 3.6 %copy-start = (bf16[256,1024]{1,0:T(8,128)(2,1)S(1)}, bf16[256,1024]{1,0:T(8,128)(2,1)}, u32[]{:S(2)}) copy-start(bf16[256,1024]{1,0:T(8,128)(2,1)} %q_hbm.1) | copy-start | bytes 1572868
  5.1 3.6 %copy-start.1 = (f32[1024]{0:T(1024)S(1)}, f32[1024]{0:T(1024)}, u32[]{:S(2)}) copy-start(f32[1024]{0:T(1024)} %param.12) | copy-start | bytes 12292

commit v4 on v3

--- a/solution.py
+++ b/solution.py
@@ -22,10 +22,10 @@
 
 
 def kernel(
-    q_hbm, c_hbm, gain_ref, win_hbm, wout_hbm, proj_hbm, code_ref, mine_ref, idx_ref, pos_ref,
+    q_hbm, c_hbm, gain_hbm, win_hbm, wout_hbm, proj_hbm, pos_hbm, asked_hbm, row_hbm, dest_hbm,
     loss_ref, grad_ref, index_ref,
     x, win, wout, proj, woutp, normed, hidden, cpart, qpart, base, crecv, qrecv,
-    codes, column, onehots, packed, embc, embq, sumq,
+    gain, pos, asked, row_of, dest, idx, codes, column, onehots, packed, embc, embq, sumq,
     fetch, cands, qall, slots, pieces, pieces_in, sums, sums_in, draw, draws, gshare, gshare_in,
     load_sem, c_s, c_r, qp_s, qp_r, code_s, code_r, col_s, col_r, plane_s, plane_r,
     fetch_s, fetch_r, q_s, q_r, piece_s, piece_r, idx_s, idx_r, sums_s, sums_r, draw_s, draw_r, grad_s, grad_r,
@@ -61,7 +61,13 @@
     load_in = pltpu.make_async_copy(win_hbm, win, load_sem.at[9])
     load_out = pltpu.make_async_copy(wout_hbm, wout, load_sem.at[10])
     load_proj = pltpu.make_async_copy(proj_hbm, proj, load_sem.at[11])
+    load_small = [
+        pltpu.make_async_copy(src, dst, load_sem.at[12 + k])
+        for k, (src, dst) in enumerate((
+            (gain_hbm, gain), (asked_hbm, asked), (row_hbm, row_of), (dest_hbm, dest), (pos_hbm, pos)))
+    ]
     load_x(0).start()
+    load_small[0].start()
     load_out.start()
     load_proj.start()
     load_in.start()
@@ -69,6 +75,9 @@
     for i in range(2, 9):
         load_x(i).start()
 
+    for load in load_small[1:]:
+        load.start()
+
     barrier = pltpu.get_barrier_semaphore()
 
     @pl.loop(1, 32)
@@ -80,10 +89,10 @@
         pl.semaphore_signal(barrier, inc=1, device_id={"mp": up(s)}, device_id_type=MESH)
 
     def code_copy(to, frm):
-        return remote(code_ref.at[0], codes.at[d, frm], code_s.at[to], code_r.at[frm], {"mp": to})
+        return remote(codes.at[d, frm], codes.at[d, frm], code_s.at[to], code_r.at[frm], {"mp": to})
 
     def column_copy(to, frm):
-        return remote(mine_ref, column.at[frm], col_s.at[to], col_r.at[frm], {"mp": to})
+        return remote(column.at[frm], column.at[frm], col_s.at[to], col_r.at[frm], {"mp": to})
 
     def plane_copy(to, frm):
         return remote(codes.at[frm], codes.at[frm], plane_s.at[to], plane_r.at[frm], {"dp": to})
@@ -151,65 +160,93 @@
         c_unit(0, u)
         c_unit(1, u)
 
+    def normalise(i, slot):
+        for r in range(0, 256, 32):
+            v = x[i, r:r + 32, :].astype(f32)
+            scale = lax.rsqrt(jnp.mean(v * v, axis=-1, keepdims=True) + norm_eps)
+            normed[slot, r:r + 32, :] = (v * scale * gain[...]).astype(bf16)
+
+    def index_places():
+        for load in load_small[1:]:
+            load.wait()
+        sub = lax.broadcasted_iota(jnp.int32, (256, 256), 0)
+        lane = lax.broadcasted_iota(jnp.int32, (256, 256), 1)
+        spread = jnp.where((lane[0:32] & 31) == sub[0:32], 1.0, 0.0).astype(bf16)
+        of_row = (lane[0:8] >> 5) == sub[0:8]
+
+        def flat(block):
+            wide = jnp.dot(block.astype(f32).astype(bf16), spread, preferred_element_type=f32)
+            return jnp.sum(jnp.where(of_row, wide, 0.0), axis=0, keepdims=True)
+
+        def rank(row, earlier):
+            column_form = jnp.sum(jnp.where(lane == sub, row, 0.0), axis=1, keepdims=True)
+            return jnp.sum(jnp.where((column_form == row) & earlier, 1.0, 0.0), axis=0, keepdims=True)
+
+        owners = flat(asked[...])
+        slot = owners * 8.0 + rank(owners, (sub & 31) < (lane & 31))
+        code = (slot * 256.0 + flat(row_of[...])).astype(jnp.int32)
+        codes[d, z] = code
+        mine = jnp.zeros((32, 128), jnp.int32)
+        for k in range(8):
+            of_k = jnp.sum(jnp.where(lane[0:32] - k * 32 == sub[0:32], code, 0), axis=1, keepdims=True)
+            mine = jnp.where(lane[0:32, 0:128] == k, of_k, mine)
+        column[z] = mine
+        goal = dest[...].astype(f32)
+        idx[...] = (goal * 16.0 + rank(goal, sub < lane)).astype(jnp.int32)
+
+    load_x(0).wait()
+    load_small[0].wait()
     load_out.wait()
     load_proj.wait()
+    normalise(0, 0)
     woutp[...] = jnp.dot(wout[...], proj[...], preferred_element_type=f32).astype(bf16)
+    load_in.wait()
 
     @pl.loop(0, 9)
     def _(i):
+        @pl.when(i == 0)
+        def _():
+            load_q.wait()
+
+        @pl.when(jnp.logical_and(i > 0, i < 8))
+        def _():
+            load_x(i + 1).wait()
+
+        slot = lax.rem(i, 2)
+        for n in range(2):
+            rows = normed[slot]
+            gate = jnp.dot(rows, win[:, n * 256:(n + 1) * 256], preferred_element_type=f32)
+            upper = jnp.dot(rows, win[:, 512 + n * 256:768 + n * 256], preferred_element_type=f32)
+            hidden[:, n * 256:(n + 1) * 256] = (gate / (1.0 + jnp.exp(-gate)) * upper).astype(bf16)
+        normalise(jnp.minimum(i + 1, 8), 1 - slot)
+
+        @pl.when(i == 0)
+        def _():
+            pl.semaphore_wait(barrier, 38)
+
         @pl.when(i == 1)
         def _():
-            load_q.wait()
-
-        @pl.when(i != 1)
-        def _():
-            load_x(i).wait()
-
-        @pl.loop(0, 8)
-        def _(r):
-            rows = pl.ds(pl.multiple_of(r * 32, 32), 32)
-            v = x[i, rows, :].astype(f32)
-            scale = lax.rsqrt(jnp.mean(v * v, axis=-1, keepdims=True) + norm_eps)
-            normed[rows, :] = (v * scale * gain_ref[...]).astype(bf16)
-
-        @pl.when(i == 0)
-        def _():
-            load_in.wait()
-
-        for n in range(2):
-            gate = jnp.dot(normed[...], win[:, n * 256:(n + 1) * 256], preferred_element_type=f32)
-            upper = jnp.dot(normed[...], win[:, 512 + n * 256:768 + n * 256], preferred_element_type=f32)
-            hidden[:, n * 256:(n + 1) * 256] = (gate / (1.0 + jnp.exp(-gate)) * upper).astype(bf16)
-
-        @pl.when(i == 0)
-        def _():
-            pl.semaphore_wait(barrier, 38)
-
-        @pl.when(i == 1)
-        def _():
-            normed[...] = jnp.dot(hidden[...], wout[...], preferred_element_type=f32).astype(bf16)
+            normed[1] = jnp.dot(hidden[...], wout[...], preferred_element_type=f32).astype(bf16)
             for k in (0, 2, 3, 4, 5, 6, 7, 8):
                 h = home_of(jnp.int32(k))
-                qpart[k] = normed[pl.ds(pl.multiple_of(h * 32, 32), 32), :]
+                qpart[k] = normed[1, pl.ds(pl.multiple_of(h * 32, 32), 32), :]
             q_unit(0, 0)
             q_unit(1, 0)
-
-        @pl.when(i != 1)
-        def _():
-            cpart[i] = jnp.dot(hidden[...], woutp[...], preferred_element_type=f32).astype(bf16)
-
-        @pl.when(i == 0)
-        def _():
-            c_unit(0, 0)
-            c_unit(1, 0)
+            index_places()
 
             @pl.loop(1, 8)
             def _(s):
                 code_copy(up(s), z).start()
                 column_copy(up(s), z).start()
 
-            codes[d, z] = code_ref[0]
-            column[z] = mine_ref[...]
+        @pl.when(i != 1)
+        def _():
+            cpart[i] = jnp.dot(hidden[...], woutp[...], preferred_element_type=f32).astype(bf16)
+
+        @pl.when(i == 0)
+        def _():
+            c_unit(0, 0)
+            c_unit(1, 0)
 
         @pl.when(i == 2)
         def _():
@@ -323,11 +360,13 @@
     @pl.loop(0, 2)
     def _(s):
         row = lax.broadcasted_iota(jnp.int32, (256, 256), 0) + s * 256
-        onehot = jnp.where(row == idx_ref[...], 1.0, 0.0).astype(bf16)
+        onehot = jnp.where(row == idx[...], 1.0, 0.0).astype(bf16)
         rows = jnp.dot(onehot, embc[...], preferred_element_type=f32).astype(bf16)
         slots[pl.ds(s * 16, 16)] = rows.reshape(16, 16, 768)
 
-    at_pos = lax.broadcasted_iota(jnp.int32, (32, 256), 1) == pos_ref[...]
+    diagonal = lax.broadcasted_iota(jnp.int32, (32, 32), 0) == lax.broadcasted_iota(jnp.int32, (32, 32), 1)
+    pos_column = jnp.sum(jnp.where(diagonal, pos[...], 0), axis=1, keepdims=True)
+    at_pos = lax.broadcasted_iota(jnp.int32, (32, 256), 1) == pos_column
     positive = jnp.dot(jnp.where(at_pos, 1.0, 0.0).astype(bf16), embc[...], preferred_element_type=f32)
     pos_score = score_scale * jnp.sum(embq[...].astype(f32) * positive, axis=1, keepdims=True)
     pos_weight = jnp.exp(pos_score)
@@ -351,10 +390,10 @@
         row = lax.broadcasted_iota(jnp.int32, (64, 256), 0)
         lane = lax.broadcasted_iota(jnp.int32, (64, 256), 1)
         slot = ((lane >> 4) * 8 + z) * 8 + (lane & 7)
-        asked = column[pl.ds(pair * 2, 2)].reshape(64, 8)
-        hit = (asked[:, 0:1] >> 8) == slot
+        wants = column[pl.ds(pair * 2, 2)].reshape(64, 128)
+        hit = (wants[:, 0:1] >> 8) == slot
         for k in range(1, 8):
-            hit = hit | ((asked[:, k:k + 1] >> 8) == slot)
+            hit = hit | ((wants[:, k:k + 1] >> 8) == slot)
         hit = hit & ((row >> 5) == ((lane >> 3) & 1))
         weight = jnp.where(hit, jnp.exp(score), 0.0)
         total = jnp.sum(weight, axis=1, keepdims=True)
@@ -387,7 +426,6 @@
         gathered = gathered + sums_in[m].astype(f32)
     total = gathered[:, 768:769] + gathered[:, 832:833] + pos_weight
     loss = jnp.log(total) - pos_score
-    diagonal = lax.broadcasted_iota(jnp.int32, (32, 32), 0) == lax.broadcasted_iota(jnp.int32, (32, 32), 1)
     loss_ref[...] = jnp.sum(jnp.where(diagonal, loss, 0.0), axis=0, keepdims=True)
     dunit = score_scale * ((gathered[:, 0:768] + pos_weight * positive) / total - positive)
     along = jnp.sum(unit * dunit, axis=1, keepdims=True)
@@ -460,7 +498,7 @@
     grad_ref[:, 384:768] = grad[4:8]
 
 
-def fused(queries, clips, gain, win, wout, proj, code, mine, idx, pos):
+def fused(*args):
     hbm = pl.BlockSpec(memory_space=pl.ANY)
     vmem = pl.BlockSpec(memory_space=pltpu.VMEM)
     sds = jax.ShapeDtypeStruct
@@ -468,7 +506,7 @@
     return pl.pallas_call(
         kernel,
         out_shape=(sds((1, 32), f32), sds((4, 768), f32), sds((32, 16, 768), bf16)),
-        in_specs=[hbm, hbm, vmem, hbm, hbm, hbm, vmem, vmem, vmem, vmem],
+        in_specs=[hbm] * 10,
         out_specs=[vmem, vmem, hbm],
         scratch_shapes=[
             pltpu.VMEM((9, 256, 1024), bf16),
@@ -476,15 +514,21 @@
             pltpu.VMEM((512, 1024), bf16),
             pltpu.VMEM((1024, 768), bf16),
             pltpu.VMEM((512, 768), bf16),
-            pltpu.VMEM((256, 1024), bf16),
+            pltpu.VMEM((2, 256, 1024), bf16),
             pltpu.VMEM((256, 512), bf16),
             pltpu.VMEM((9, 256, 768), bf16),
             pltpu.VMEM((9, 32, 1024), bf16),
             pltpu.VMEM((256, 768), f32),
             pltpu.VMEM((2, 7, 128, 768), bf16),
             pltpu.VMEM((2, 7, 16, 1024), bf16),
+            pltpu.VMEM((1, 1024), f32),
+            pltpu.VMEM((1, 32), jnp.int32),
+            pltpu.VMEM((8, 32), jnp.int32),
+            pltpu.VMEM((8, 32), jnp.int32),
+            pltpu.VMEM((1, 256), jnp.int32),
+            pltpu.VMEM((1, 256), jnp.int32),
             pltpu.VMEM((16, 8, 1, 256), jnp.int32),
-            pltpu.VMEM((8, 32, 8), jnp.int32),
+            pltpu.VMEM((8, 32, 128), jnp.int32),
             pltpu.VMEM((4, 256, 256), bf16),
             pltpu.VMEM((256, 256), f32),
             pltpu.VMEM((256, 768), bf16),
@@ -502,7 +546,7 @@
             pltpu.VMEM((8, 32, 768), bf16),
             pltpu.VMEM((32, 8, 384), f32),
             pltpu.VMEM((32, 8, 384), f32),
-            dma((12,)), dma((2, 7)), dma((2, 7)), dma((2, 7)), dma((2, 7)), dma((8,)), dma((8,)), dma((8,)), dma((8,)),
+            dma((17,)), dma((2, 7)), dma((2, 7)), dma((2, 7)), dma((2, 7)), dma((8,)), dma((8,)), dma((8,)), dma((8,)),
             dma((16,)), dma((16,)), dma((4, 16)), dma((4, 16)), dma((8,)), dma((8,)), dma((8,)), dma((8,)),
             dma((32,)), dma((32,)), dma((8,)), dma((8,)), dma((8,)), dma((8,)), dma((32,)), dma((32,)),
         ],
@@ -510,26 +554,16 @@
             collective_id=0, has_side_effects=True, vmem_limit_bytes=52 * 1024 * 1024),
         cost_estimate=pl.CostEstimate(flops=11_000_000_000, bytes_accessed=20_000_000, transcendentals=2_000_000),
         name="fused",
-    )(queries, clips, gain, win, wout, proj, code, mine, idx, pos)
-
-
-def ranks_of(ids):
-    count = ids.shape[0]
-    earlier = jnp.arange(count)[None, :] < jnp.arange(count)[:, None]
-    return jnp.sum(((ids[:, None] == ids[None, :]) & earlier).astype(jnp.int32), axis=1)
+    )(*args)
 
 
 def per_device(
     queries, clips, norm_gain, w_in, w_out, proj, pos_row, neg_owner, neg_row, clip_dest
 ):
     width = queries.shape[1]
-    asked = neg_owner.reshape(-1)
-    code = (asked * 8 + ranks_of(asked)) * 256 + neg_row.reshape(-1)
-    destination = clip_dest[:, 0]
-    idx = destination * 16 + ranks_of(destination)
     loss, grad, index = fused(
         queries, clips, norm_gain.reshape(1, width), w_in.reshape(width, -1), w_out, proj,
-        code.reshape(1, 1, -1), code.reshape(neg_owner.shape), idx.reshape(1, -1), pos_row.reshape(-1, 1))
+        pos_row.reshape(1, -1), neg_owner.T, neg_row.T, clip_dest.reshape(1, -1))
     return (loss.reshape(-1), index.reshape(-1, index.shape[-1]), grad)
 
 

time: 108 us -> 103 us (0.954)
  local copies, waits for them, and re-layouts: 8.18 us -> 5.58 us
  other arithmetic: 1.83 us -> 0 us
    unnamed x10 -> x16, local copies, waits for them, and re-layouts: 7.1 us -> 5.58 us
    reduce_sum x2 -> x0, other arithmetic: 1.11 us -> none  [ranks_of(): jnp.sum(((ids[:, None] == ids[None, :]) & earlier).astype(jnp.int32), axi...]
where the time goes in v4:
time: 103 us
  Pallas kernels  96.3 us (93%)
  local copies, waits for them, and re-layouts  5.58 us (5%)
    pallas_call x1, Pallas kernels, fused(): pl.pallas_call(kernel, out_shape=(sds((1, 32), f32), sds((4, 768), f32),...  96.3 us
    unnamed x16, local copies, waits for them, and re-layouts  5.58 us

profile of v4, /device:TPU:1, one launch (start us, length us, event | category | flops | bytes accessed | tf_op | source)
XLA Modules:
  0.0 102.6 jit_solution(6893314910172164498)
XLA Ops:
  0.6 0.0 copy-start
  0.6 0.0 copy-start.1
  0.7 0.0 copy-start.2
  0.7 0.0 copy-start.3
  0.7 0.0 copy-start.4
  0.7 0.0 copy-start.5
  0.7 3.6 %copy.13 = bf16[128,8,2,512]{3,1,2,0:T(8,128)(2,1)} copy(bf16[128,8,2,512]{3,2,1,0:T(2,128)(2,1)} %bitcast.16) | data formatting | bytes 4194304
  4.3 0.0 copy-done
  4.3 0.0 copy-done.1
  4.3 0.0 copy-done.2
  4.3 0.0 copy-done.3
  4.3 0.0 copy-done.4
  4.3 0.0 copy-done.5
  4.3 96.3 %fused.1 = (f32[1,32]{1,0:T(1,128)S(1)}, f32[4,768]{1,0:T(4,128)S(1)}, bf16[32,16,768]{2,1,0:T(8,128)(2,1)S(1)}) custom-call(bf16[256,1024]{1,0:T(8,128)(2,1)S(1)} %copy-done, bf16[2048,1024]{1,0:T(8,128)(2,1)} %c_hbm.1, f32[1,1024]{1,0:T(1,128)S(1)} %bitcast.10, bf16[1024,1024]{1,0:T(8,128)(2,1)} %bitcast.17, bf16[512,1024]{1,0:T(8,128)(2,1)} %wout_hbm.1, ...), custom_call_target="tpu_custom_call" | custom-call | flops 11000000512 | bytes 20000000 | tf_op jit(solution)/shard_map/fused/pallas_call | solution.py:506
  100.6 0.5 copy.17
  101.1 0.9 copy.18
  102.0 0.6 copy.19
Async XLA Ops:
  0.6 3.6 %copy-start = (bf16[256,1024]{1,0:T(8,128)(2,1)S(1)}, bf16[256,1024]{1,0:T(8,128)(2,1)}, u32[]{:S(2)}) copy-start(bf16[256,1024]{1,0:T(8,128)(2,1)} %q_hbm.1) | copy-start | bytes 1572868
  0.6 3.6 %copy-start.1 = (f32[1024]{0:T(1024)S(1)}, f32[1024]{0:T(1024)}, u32[]{:S(2)}) copy-start(f32[1024]{0:T(1024)} %param.12) | copy-start | bytes 12292
  0.7 3.6 %copy-start.2 = (s32[32,8]{0,1:T(8,128)S(1)}, s32[32,8]{0,1:T(8,128)}, u32[]{:S(2)}) copy-start(s32[32,8]{0,1:T(8,128)} %param.17) | copy-start | bytes 3076
  0.7 3.6 %copy-start.3 = (s32[32,8]{0,1:T(8,128)S(1)}, s32[32,8]{0,1:T(8,128)}, u32[]{:S(2)}) copy-start(s32[32,8]{0,1:T(8,128)} %param.18) | copy-start | bytes 3076
  0.7 3.6 %copy-start.4 = (s32[256,1]{0,1:T(1,128)S(1)}, s32[256,1]{0,1:T(1,128)}, u32[]{:S(2)}) copy-start(s32[256,1]{0,1:T(1,128)} %param.19) | copy-start | bytes 3076
  0.7 3.6 %copy-start.5 = (s32[32]{0:T(128)S(1)}, s32[32]{0:T(128)}, u32[]{:S(2)}) copy-start(s32[32]{0:T(128)} %param.16) | copy-start | bytes 388

commit v5 on v4

--- a/solution.py
+++ b/solution.py
@@ -27,8 +27,9 @@
     x, win, wout, proj, woutp, normed, hidden, cpart, qpart, base, crecv, qrecv,
     gain, pos, asked, row_of, dest, idx, codes, column, onehots, packed, embc, embq, sumq,
     fetch, cands, qall, slots, pieces, pieces_in, sums, sums_in, draw, draws, gshare, gshare_in,
-    load_sem, c_s, c_r, qp_s, qp_r, code_s, code_r, col_s, col_r, plane_s, plane_r,
-    fetch_s, fetch_r, q_s, q_r, piece_s, piece_r, idx_s, idx_r, sums_s, sums_r, draw_s, draw_r, grad_s, grad_r,
+    load_sem, c_s, c_r, qp_s, qp_r, q_r, fetch_s, fetch_r,
+    code_s, code_r, plane_s, plane_r, q_s, piece_s, piece_r, own_s, idx_s, idx_r, sums_s, sums_r, draw_s, draw_r,
+    grad_s, grad_r,
 ):
     g, d, z = lax.axis_index("group"), lax.axis_index("dp"), lax.axis_index("mp")
     y, xx = d // 4, lax.rem(d, 4)
@@ -89,35 +90,34 @@
         pl.semaphore_signal(barrier, inc=1, device_id={"mp": up(s)}, device_id_type=MESH)
 
     def code_copy(to, frm):
-        return remote(codes.at[d, frm], codes.at[d, frm], code_s.at[to], code_r.at[frm], {"mp": to})
-
-    def column_copy(to, frm):
-        return remote(column.at[frm], column.at[frm], col_s.at[to], col_r.at[frm], {"mp": to})
+        return remote(codes.at[d, frm], codes.at[d, frm], code_s, code_r, {"mp": to})
 
     def plane_copy(to, frm):
-        return remote(codes.at[frm], codes.at[frm], plane_s.at[to], plane_r.at[frm], {"dp": to})
+        return remote(codes.at[frm], codes.at[frm], plane_s, plane_r, {"dp": to})
 
     def q_copy(to, frm):
-        return remote(embq, qall.at[frm], q_s.at[to], q_r.at[frm], {"mp": to})
+        return remote(embq, qall.at[frm], q_s, q_r.at[frm], {"mp": to})
 
     def fetch_copy(pair, to, frm):
-        return remote(
-            fetch.at[pair, to], cands.at[pair, frm], fetch_s.at[pair, to], fetch_r.at[pair, frm], {"dp": to})
+        return remote(fetch.at[pair, to], cands.at[pair, frm], fetch_s.at[pair], fetch_r.at[pair], {"dp": to})
 
     def piece_copy(to, frm):
-        return remote(pieces.at[to // 2], pieces_in.at[frm], piece_s.at[to], piece_r.at[frm], {"mp": to})
+        return remote(pieces.at[to // 2], pieces_in.at[frm], piece_s, piece_r, {"mp": to})
 
     def index_copy(to, frm):
-        return remote(slots.at[to], index_ref.at[frm], idx_s.at[to], idx_r.at[frm], owner(to))
+        return remote(slots.at[to], index_ref.at[frm], idx_s, idx_r, owner(to))
 
     def sums_copy(to, frm):
-        return remote(sums.at[to], sums_in.at[frm], sums_s.at[to], sums_r.at[frm], {"mp": to})
+        return remote(sums.at[to], sums_in.at[frm], sums_s, sums_r, {"mp": to})
 
     def draw_copy(to, frm):
-        return remote(draw, draws.at[frm], draw_s.at[to], draw_r.at[frm], {"mp": to})
+        return remote(draw, draws.at[frm], draw_s, draw_r, {"mp": to})
 
     def grad_copy(to, frm):
-        return remote(gshare.at[to], gshare_in.at[frm], grad_s.at[to], grad_r.at[frm], owner(to))
+        return remote(gshare.at[to], gshare_in.at[frm], grad_s, grad_r, owner(to))
+
+    def wait_batch(ref, semaphore):
+        pltpu.make_async_copy(ref, ref, semaphore).wait()
 
     def spot(way, u):
         if u == 0:
@@ -126,39 +126,49 @@
             dist, half = 4 - (u + 1) // 2, 1 - way
         else:
             dist, half = 4 - u // 2, way
-        return part_of(way, dist), slice(half * 128, half * 128 + 128), slice(half * 16, half * 16 + 16)
-
-    def c_copy(way, u):
-        i, rows, _ = spot(way, u)
+        return part_of(way, dist), half
+
+    def c_copy(way, n):
+        i, half = spot(way, n // 2)
+        start = half * 128 + n % 2 * 64
         return remote(
-            cpart.at[i, rows], crecv.at[way, u], c_s.at[way, u], c_r.at[way, u],
+            cpart.at[i, start:start + 64], crecv.at[way, n], c_s.at[way, n % 2], c_r.at[way, n],
             {"mp": right if way == 0 else left})
 
     def qp_copy(way, u):
-        i, _, rows = spot(way, u)
+        i, half = spot(way, u)
         return remote(
-            qpart.at[i, rows], qrecv.at[way, u], qp_s.at[way, u], qp_r.at[way, u],
+            qpart.at[i, half * 16:half * 16 + 16], qrecv.at[way, u], qp_s.at[way, u % 2], qp_r.at[way, u],
             {"mp": right if way == 0 else left})
 
     def q_unit(way, u):
-        i, _, rows = spot(way, u)
+        i, half = spot(way, u)
+        rows = slice(half * 16, half * 16 + 16)
         if u >= 2:
             qp_copy(way, u - 2).wait_recv()
             qpart[i, rows] = (qpart[i, rows].astype(f32) + qrecv[way, u - 2].astype(f32)).astype(bf16)
+            qp_copy(way, u - 2).wait_send()
         qp_copy(way, u).start()
 
-    def c_unit(way, u):
-        i, rows, _ = spot(way, u)
-        if u >= 2:
-            c_copy(way, u - 2).wait_recv()
-            cpart[i, rows] = (cpart[i, rows].astype(f32) + crecv[way, u - 2].astype(f32)).astype(bf16)
-        c_copy(way, u).start()
+    def c_unit(way, n):
+        i, half = spot(way, n // 2)
+        rows = slice(half * 128 + n % 2 * 64, half * 128 + n % 2 * 64 + 64)
+        if n >= 4:
+            c_copy(way, n - 4).wait_recv()
+            cpart[i, rows] = (cpart[i, rows].astype(f32) + crecv[way, n - 4].astype(f32)).astype(bf16)
+        if n >= 2:
+            c_copy(way, n - 2).wait_send()
+        c_copy(way, n).start()
+
+    def c_units(u):
+        for n in (2 * u, 2 * u + 1):
+            c_unit(0, n)
+            c_unit(1, n)
 
     def both_units(u):
         q_unit(0, u)
         q_unit(1, u)
-        c_unit(0, u)
-        c_unit(1, u)
+        c_units(u)
 
     def normalise(i, slot):
         for r in range(0, 256, 32):
@@ -186,11 +196,6 @@
         slot = owners * 8.0 + rank(owners, (sub & 31) < (lane & 31))
         code = (slot * 256.0 + flat(row_of[...])).astype(jnp.int32)
         codes[d, z] = code
-        mine = jnp.zeros((32, 128), jnp.int32)
-        for k in range(8):
-            of_k = jnp.sum(jnp.where(lane[0:32] - k * 32 == sub[0:32], code, 0), axis=1, keepdims=True)
-            mine = jnp.where(lane[0:32, 0:128] == k, of_k, mine)
-        column[z] = mine
         goal = dest[...].astype(f32)
         idx[...] = (goal * 16.0 + rank(goal, sub < lane)).astype(jnp.int32)
 
@@ -237,7 +242,6 @@
             @pl.loop(1, 8)
             def _(s):
                 code_copy(up(s), z).start()
-                column_copy(up(s), z).start()
 
         @pl.when(i != 1)
         def _():
@@ -245,18 +249,11 @@
 
         @pl.when(i == 0)
         def _():
-            c_unit(0, 0)
-            c_unit(1, 0)
-
-        @pl.when(i == 2)
-        def _():
-            q_unit(0, 1)
-            c_unit(0, 1)
+            c_units(0)
 
         @pl.when(i == 3)
         def _():
-            q_unit(1, 1)
-            c_unit(1, 1)
+            both_units(1)
 
         @pl.when(i == 5)
         def _():
@@ -264,21 +261,19 @@
 
         @pl.when(i == 6)
         def _():
-            @pl.loop(1, 8)
-            def _(s):
-                code_copy(z, up(s)).wait_recv()
-                column_copy(z, up(s)).wait_recv()
+            wait_batch(codes.at[d, 0:7], code_r)
 
             @pl.loop(1, 16)
             def _(s):
                 plane_copy(lax.rem(d + s, 16), d).start()
 
-    both_units(3)
+        @pl.when(i == 7)
+        def _():
+            both_units(3)
+
     base[...] = jnp.dot(x[8], proj[...], preferred_element_type=f32) + cpart[8].astype(f32)
-
-    @pl.loop(1, 16)
-    def _(s):
-        plane_copy(d, lax.rem(d + s, 16)).wait_recv()
+    both_units(4)
+    wait_batch(codes.at[0:15], plane_r)
 
     owner_slot = (d * 8 + z) * 8
 
@@ -293,17 +288,23 @@
                 packed[c * 16 + k * 8:c * 16 + k * 8 + 8, :] = jnp.where(lane == row, 1.0, 0.0)
         onehots[pair] = packed[...].astype(bf16)
 
-    @pl.loop(0, 2)
+    @pl.loop(0, 4)
     def _(pair):
         wanted(pair)
 
-    both_units(4)
-
-    @pl.loop(2, 4)
-    def _(pair):
-        wanted(pair)
-
     both_units(5)
+
+    @pl.loop(0, 8)
+    def _(m):
+        sub = lax.broadcasted_iota(jnp.int32, (32, 256), 0)
+        lane = lax.broadcasted_iota(jnp.int32, (32, 256), 1)
+        code = codes[d, m]
+        wants = jnp.zeros((32, 128), jnp.int32)
+        for k in range(8):
+            of_k = jnp.sum(jnp.where(lane - k * 32 == sub, code, 0), axis=1, keepdims=True)
+            wants = jnp.where(lane[:, 0:128] == k, of_k, wants)
+        column[m] = wants
+
     both_units(6)
 
     for way in (0, 1):
@@ -324,27 +325,34 @@
         q_copy(up(s), z).start()
 
     for way in (0, 1):
-        for u in (5, 6):
-            c_copy(way, u).wait_recv()
+        for n in (10, 11, 12, 13):
+            c_copy(way, n).wait_recv()
     for half in range(2):
-        for r in range(0, 128, 64):
-            rows = slice(half * 128 + r, half * 128 + r + 64)
+        for r in range(2):
+            rows = slice(half * 128 + r * 64, half * 128 + r * 64 + 64)
             raw_c = (
-                base[rows, :] + crecv[0, 6 - half, r:r + 64].astype(f32)
-                + crecv[1, 5 + half, r:r + 64].astype(f32))
+                base[rows, :] + crecv[0, 12 - 2 * half + r].astype(f32) + crecv[1, 10 + 2 * half + r].astype(f32))
             inverse = lax.rsqrt(jnp.sum(raw_c * raw_c, axis=-1, keepdims=True) + embed_eps)
             embc[rows, :] = (raw_c * inverse).astype(bf16)
 
     def pair_at(s):
         return lax.rem(z // 2 + 1 + s, 4)
+
+    def send_fetch(s):
+        pair = pair_at(s)
+        for dy, dx in FAR_FIRST:
+            fetch_copy(pair, across(dy, dx), d).start()
 
     @pl.loop(0, 4)
     def _(s):
         pair = pair_at(s)
         rows = jnp.dot(onehots[pair], embc[...], preferred_element_type=f32).astype(bf16)
         fetch[pair] = rows.reshape(16, 16, 768)
-        for dy, dx in FAR_FIRST:
-            fetch_copy(pair, across(dy, dx), d).start()
+
+        @pl.when(s == 0)
+        def _():
+            send_fetch(0)
+
         cands[pair, d] = fetch[pair, d]
 
     turned = sumq[...].astype(f32).T.reshape(32, 4, 8, 32)
@@ -371,17 +379,22 @@
     pos_score = score_scale * jnp.sum(embq[...].astype(f32) * positive, axis=1, keepdims=True)
     pos_weight = jnp.exp(pos_score)
 
+    send_fetch(1)
+
     @pl.loop(0, 4)
     def _(s):
         pair = pair_at(s)
+        wait_batch(cands.at[pair, 0:15], fetch_r.at[pair])
+        wait_batch(fetch.at[pair, 0:15], fetch_s.at[pair])
+
+        @pl.when(s < 2)
+        def _():
+            send_fetch(s + 2)
+
         for k in range(2):
             @pl.when(pair * 2 + k != z)
             def _():
                 q_copy(z, pair * 2 + k).wait_recv()
-
-        @pl.loop(1, 16)
-        def _(t):
-            fetch_copy(pair, d, lax.rem(d + t, 16)).wait_recv()
 
         q = qall[pl.ds(pair * 2, 2)].reshape(64, 768)
         cand = cands[pair].reshape(256, 768)
@@ -410,16 +423,14 @@
                 sums_copy(pair * 2 + k, z).start()
 
     sums_in[z] = sums[z]
-    own_index = pltpu.make_async_copy(slots.at[here], index_ref.at[here], idx_s.at[here])
+    own_index = pltpu.make_async_copy(slots.at[here], index_ref.at[here], own_s)
     own_index.start()
     for dy, dx in FAR_FIRST:
         for k in range(2):
             index_copy(k * 16 + across(dy, dx), here).start()
     index_copy((1 - g) * 16 + d, here).start()
 
-    @pl.loop(1, 8)
-    def _(s):
-        sums_copy(z, up(s)).wait_recv()
+    wait_batch(sums_in.at[0:7], sums_r)
 
     gathered = sums_in[0].astype(f32)
     for m in range(1, 8):
@@ -434,13 +445,8 @@
         draw_copy(up(s), z).start()
     draws[z] = draw[...]
 
-    @pl.loop(1, 8)
-    def _(s):
-        piece_copy(z, up(s)).wait_recv()
-
-    @pl.loop(1, 8)
-    def _(s):
-        draw_copy(z, up(s)).wait_recv()
+    wait_batch(pieces_in.at[0:7], piece_r)
+    wait_batch(draws.at[0:7], draw_r)
 
     term = lax.dot_general(
         pieces_in[...].reshape(256, 256), draws[...].reshape(256, 768), (((0,), (0,)), ((), ())),
@@ -459,40 +465,21 @@
     gshare_in[here] = gshare[here]
 
     for way in (0, 1):
-        for u in range(7):
+        for u in (5, 6):
             qp_copy(way, u).wait_send()
-            c_copy(way, u).wait_send()
-
-    @pl.loop(1, 8)
-    def _(s):
-        code_copy(up(s), z).wait_send()
-        column_copy(up(s), z).wait_send()
-        q_copy(up(s), z).wait_send()
-        piece_copy(up(s), z).wait_send()
-        sums_copy(up(s), z).wait_send()
-        draw_copy(up(s), z).wait_send()
-
-    @pl.loop(1, 16)
-    def _(s):
-        to = lax.rem(d + s, 16)
-        plane_copy(to, d).wait_send()
-        for pair in range(4):
-            fetch_copy(pair, to, d).wait_send()
-
+        for n in (12, 13):
+            c_copy(way, n).wait_send()
+    wait_batch(codes.at[d, 0:7], code_s)
+    wait_batch(codes.at[0:15], plane_s)
+    wait_batch(qall.at[0:7], q_s)
+    wait_batch(pieces_in.at[0:7], piece_s)
+    wait_batch(sums.at[0:7], sums_s)
+    wait_batch(draws.at[0:7], draw_s)
     own_index.wait()
-
-    @pl.loop(1, 32)
-    def _(s):
-        other = lax.rem(here + s, 32)
-        index_copy(other, here).wait_send()
-        index_copy(here, other).wait_recv()
-
-    @pl.loop(1, 32)
-    def _(s):
-        other = lax.rem(here + s, 32)
-        grad_copy(other, here).wait_send()
-        grad_copy(here, other).wait_recv()
-
+    wait_batch(slots.at[0:31], idx_s)
+    wait_batch(index_ref.at[0:31], idx_r)
+    wait_batch(gshare.at[0:31], grad_s)
+    wait_batch(gshare_in.at[0:31], grad_r)
     grad = jnp.sum(gshare_in[...], axis=0)
     grad_ref[:, 0:384] = grad[0:4]
     grad_ref[:, 384:768] = grad[4:8]
@@ -519,7 +506,7 @@
             pltpu.VMEM((9, 256, 768), bf16),
             pltpu.VMEM((9, 32, 1024), bf16),
             pltpu.VMEM((256, 768), f32),
-            pltpu.VMEM((2, 7, 128, 768), bf16),
+            pltpu.VMEM((2, 14, 64, 768), bf16),
             pltpu.VMEM((2, 7, 16, 1024), bf16),
             pltpu.VMEM((1, 1024), f32),
             pltpu.VMEM((1, 32), jnp.int32),
@@ -546,9 +533,8 @@
             pltpu.VMEM((8, 32, 768), bf16),
             pltpu.VMEM((32, 8, 384), f32),
             pltpu.VMEM((32, 8, 384), f32),
-            dma((17,)), dma((2, 7)), dma((2, 7)), dma((2, 7)), dma((2, 7)), dma((8,)), dma((8,)), dma((8,)), dma((8,)),
-            dma((16,)), dma((16,)), dma((4, 16)), dma((4, 16)), dma((8,)), dma((8,)), dma((8,)), dma((8,)),
-            dma((32,)), dma((32,)), dma((8,)), dma((8,)), dma((8,)), dma((8,)), dma((32,)), dma((32,)),
+            dma((17,)), dma((2, 2)), dma((2, 14)), dma((2, 2)), dma((2, 7)), dma((8,)), dma((4,)), dma((4,)),
+            *[dma] * 16,
         ],
         compiler_params=pltpu.CompilerParams(
             collective_id=0, has_side_effects=True, vmem_limit_bytes=52 * 1024 * 1024),

time: 103 us -> 96.4 us (0.936)
  Pallas kernels: 96.3 us -> 90 us
    pallas_call x1, Pallas kernels: 96.3 us -> 90 us  [fused(): pl.pallas_call(kernel, out_shape=(sds((1, 32), f32), sds((4, 768), f32),...]
where the time goes in v5:
time: 96.4 us; the launch traced here: 96.3 us
  Pallas kernels  90 us (93%)
  local copies, waits for them, and re-layouts  5.58 us (6%)
    pallas_call x1, Pallas kernels, fused(): pl.pallas_call(kernel, out_shape=(sds((1, 32), f32), sds((4, 768), f32),...  90 us
    unnamed x16, local copies, waits for them, and re-layouts  5.58 us

profile of v5, /device:TPU:1, one launch (start us, length us, event | category | flops | bytes accessed | tf_op | source)
XLA Modules:
  0.0 96.3 jit_solution(7042011728391698814)
XLA Ops:
  0.6 0.0 copy-start
  0.6 0.0 copy-start.1
  0.7 0.0 copy-start.2
  0.7 0.0 copy-start.3
  0.7 0.0 copy-start.4
  0.7 0.0 copy-start.5
  0.7 3.6 %copy.13 = bf16[128,8,2,512]{3,1,2,0:T(8,128)(2,1)} copy(bf16[128,8,2,512]{3,2,1,0:T(2,128)(2,1)} %bitcast.16) | data formatting | bytes 4194304
  4.3 0.0 copy-done
  4.3 0.0 copy-done.1
  4.3 0.0 copy-done.2
  4.3 0.0 copy-done.3
  4.3 0.0 copy-done.4
  4.3 0.0 copy-done.5
  4.3 90.0 %fused.1 = (f32[1,32]{1,0:T(1,128)S(1)}, f32[4,768]{1,0:T(4,128)S(1)}, bf16[32,16,768]{2,1,0:T(8,128)(2,1)S(1)}) custom-call(bf16[256,1024]{1,0:T(8,128)(2,1)S(1)} %copy-done, bf16[2048,1024]{1,0:T(8,128)(2,1)} %c_hbm.1, f32[1,1024]{1,0:T(1,128)S(1)} %bitcast.10, bf16[1024,1024]{1,0:T(8,128)(2,1)} %bitcast.17, bf16[512,1024]{1,0:T(8,128)(2,1)} %wout_hbm.1, ...), custom_call_target="tpu_custom_call" | custom-call | flops 11000000512 | bytes 20000000 | tf_op jit(solution)/shard_map/fused/pallas_call | solution.py:493
  94.3 0.5 copy.17
  94.9 0.9 copy.18
  95.7 0.6 copy.19
Async XLA Ops:
  0.6 3.6 %copy-start = (bf16[256,1024]{1,0:T(8,128)(2,1)S(1)}, bf16[256,1024]{1,0:T(8,128)(2,1)}, u32[]{:S(2)}) copy-start(bf16[256,1024]{1,0:T(8,128)(2,1)} %q_hbm.1) | copy-start | bytes 1572868
  0.6 3.6 %copy-start.1 = (f32[1024]{0:T(1024)S(1)}, f32[1024]{0:T(1024)}, u32[]{:S(2)}) copy-start(f32[1024]{0:T(1024)} %param.12) | copy-start | bytes 12292
  0.7 3.6 %copy-start.2 = (s32[32,8]{0,1:T(8,128)S(1)}, s32[32,8]{0,1:T(8,128)}, u32[]{:S(2)}) copy-start(s32[32,8]{0,1:T(8,128)} %param.17) | copy-start | bytes 3076
  0.7 3.6 %copy-start.3 = (s32[32,8]{0,1:T(8,128)S(1)}, s32[32,8]{0,1:T(8,128)}, u32[]{:S(2)}) copy-start(s32[32,8]{0,1:T(8,128)} %param.18) | copy-start | bytes 3076
  0.7 3.6 %copy-start.4 = (s32[256,1]{0,1:T(1,128)S(1)}, s32[256,1]{0,1:T(1,128)}, u32[]{:S(2)}) copy-start(s32[256,1]{0,1:T(1,128)} %param.19) | copy-start | bytes 3076
  0.7 3.6 %copy-start.5 = (s32[32]{0:T(128)S(1)}, s32[32]{0:T(128)}, u32[]{:S(2)}) copy-start(s32[32]{0:T(128)} %param.16) | copy-start | bytes 388

commit v6 on v5

--- a/solution.py
+++ b/solution.py
@@ -26,10 +26,10 @@
     loss_ref, grad_ref, index_ref,
     x, win, wout, proj, woutp, normed, hidden, cpart, qpart, base, crecv, qrecv,
     gain, pos, asked, row_of, dest, idx, codes, column, onehots, packed, embc, embq, sumq,
-    fetch, cands, qall, slots, pieces, pieces_in, sums, sums_in, draw, draws, gshare, gshare_in,
+    fetch, cands, qall, slots, pieces, pieces_in, turned_in, sums, sums_in, draw, draws, gshare, gshare_in, gpart,
     load_sem, c_s, c_r, qp_s, qp_r, q_r, fetch_s, fetch_r,
     code_s, code_r, plane_s, plane_r, q_s, piece_s, piece_r, own_s, idx_s, idx_r, sums_s, sums_r, draw_s, draw_r,
-    grad_s, grad_r,
+    grad_s, grad_r, part_s, part_r,
 ):
     g, d, z = lax.axis_index("group"), lax.axis_index("dp"), lax.axis_index("mp")
     y, xx = d // 4, lax.rem(d, 4)
@@ -95,8 +95,13 @@
     def plane_copy(to, frm):
         return remote(codes.at[frm], codes.at[frm], plane_s, plane_r, {"dp": to})
 
-    def q_copy(to, frm):
-        return remote(embq, qall.at[frm], q_s, q_r.at[frm], {"mp": to})
+    def forward_q(k):
+        if k:
+            for h in (up(k), up(8 - k)):
+                wait_batch(qall.at[h], q_r.at[h])
+        for to, h, rows in ((right, up(8 - k) if k else z, pl.ds(0, 16)), (left, up(k), pl.ds(16, 16))):
+            block = qall.at[h] if k < 3 else qall.at[h, rows]
+            remote(block, block, q_s, q_r.at[h], {"mp": to}).start()
 
     def fetch_copy(pair, to, frm):
         return remote(fetch.at[pair, to], cands.at[pair, frm], fetch_s.at[pair], fetch_r.at[pair], {"dp": to})
@@ -111,7 +116,7 @@
         return remote(sums.at[to], sums_in.at[frm], sums_s, sums_r, {"mp": to})
 
     def draw_copy(to, frm):
-        return remote(draw, draws.at[frm], draw_s, draw_r, {"mp": to})
+        return remote(draw.at[lax.rem(to, 2)], draws.at[frm], draw_s, draw_r, {"mp": to})
 
     def grad_copy(to, frm):
         return remote(gshare.at[to], gshare_in.at[frm], grad_s, grad_r, owner(to))
@@ -321,14 +326,13 @@
     unit = raw / length
     embq[...] = unit.astype(bf16)
     qall[z] = embq[...]
-    for s in (6, 7, 5, 4, 3, 2, 1):
-        q_copy(up(s), z).start()
-
-    for way in (0, 1):
-        for n in (10, 11, 12, 13):
-            c_copy(way, n).wait_recv()
-    for half in range(2):
-        for r in range(2):
+    forward_q(0)
+
+    for r in range(2):
+        for way in (0, 1):
+            c_copy(way, 10 + r).wait_recv()
+            c_copy(way, 12 + r).wait_recv()
+        for half in range(2):
             rows = slice(half * 128 + r * 64, half * 128 + r * 64 + 64)
             raw_c = (
                 base[rows, :] + crecv[0, 12 - 2 * half + r].astype(f32) + crecv[1, 10 + 2 * half + r].astype(f32))
@@ -355,6 +359,8 @@
 
         cands[pair, d] = fetch[pair, d]
 
+    forward_q(1)
+
     turned = sumq[...].astype(f32).T.reshape(32, 4, 8, 32)
     for k in range(4):
         pieces[k] = turned[:, k].reshape(256, 32).T.astype(bf16)
@@ -364,6 +370,8 @@
         piece_copy(up(s), z).start()
 
     pieces_in[z] = pieces[z // 2]
+    send_fetch(1)
+    forward_q(2)
 
     @pl.loop(0, 2)
     def _(s):
@@ -379,7 +387,7 @@
     pos_score = score_scale * jnp.sum(embq[...].astype(f32) * positive, axis=1, keepdims=True)
     pos_weight = jnp.exp(pos_score)
 
-    send_fetch(1)
+    forward_q(3)
 
     @pl.loop(0, 4)
     def _(s):
@@ -391,10 +399,9 @@
         def _():
             send_fetch(s + 2)
 
-        for k in range(2):
-            @pl.when(pair * 2 + k != z)
-            def _():
-                q_copy(z, pair * 2 + k).wait_recv()
+        @pl.when(s == 1)
+        def _():
+            wait_batch(qall.at[up(4)], q_r.at[up(4)])
 
         q = qall[pl.ds(pair * 2, 2)].reshape(64, 768)
         cand = cands[pair].reshape(256, 768)
@@ -430,6 +437,8 @@
             index_copy(k * 16 + across(dy, dx), here).start()
     index_copy((1 - g) * 16 + d, here).start()
 
+    wait_batch(pieces_in.at[0:7], piece_r)
+    turned_in[...] = pieces_in[...].reshape(256, 256).astype(f32).T.astype(bf16)
     wait_batch(sums_in.at[0:7], sums_r)
 
     gathered = sums_in[0].astype(f32)
@@ -440,24 +449,16 @@
     loss_ref[...] = jnp.sum(jnp.where(diagonal, loss, 0.0), axis=0, keepdims=True)
     dunit = score_scale * ((gathered[:, 0:768] + pos_weight * positive) / total - positive)
     along = jnp.sum(unit * dunit, axis=1, keepdims=True)
-    draw[...] = ((dunit - unit * along) / length).astype(bf16)
+    drawn = ((dunit - unit * along) / length).astype(bf16)
+    draw[0] = drawn[:, 0:384]
+    draw[1] = drawn[:, 384:768]
     for s in (4, 3, 5, 2, 6, 1, 7):
         draw_copy(up(s), z).start()
-    draws[z] = draw[...]
-
-    wait_batch(pieces_in.at[0:7], piece_r)
+    parity = lax.rem(z, 2)
+    draws[z] = draw[parity]
     wait_batch(draws.at[0:7], draw_r)
-
-    term = lax.dot_general(
-        pieces_in[...].reshape(256, 256), draws[...].reshape(256, 768), (((0,), (0,)), ((), ())),
-        preferred_element_type=f32).reshape(32, 8, 768)
-    turned_term = jnp.concatenate([term[:, 4:8], term[:, 0:4]], axis=1)
-    even = lax.rem(z, 2) == 0
-    upper_rows = lax.broadcasted_iota(jnp.int32, (32, 8, 384), 1) < 4
-    gshare[...] = jnp.where(
-        upper_rows,
-        jnp.where(even, term[:, :, 0:384], turned_term[:, :, 0:384]),
-        jnp.where(even, turned_term[:, :, 384:768], term[:, :, 384:768]))
+    gshare[...] = jnp.dot(
+        turned_in[...], draws[...].reshape(256, 384), preferred_element_type=f32).reshape(32, 8, 384)
     for dy, dx in FAR_FIRST:
         for k in range(2):
             grad_copy(k * 16 + across(dy, dx), here).start()
@@ -478,11 +479,15 @@
     own_index.wait()
     wait_batch(slots.at[0:31], idx_s)
     wait_batch(index_ref.at[0:31], idx_r)
+    wait_batch(gshare_in.at[0:31], grad_r)
+    gpart[parity] = jnp.sum(gshare_in[...], axis=0)
+    swap = remote(gpart.at[parity], gpart.at[parity], part_s, part_r, {"mp": z + 1 - 2 * parity})
+    swap.start()
     wait_batch(gshare.at[0:31], grad_s)
-    wait_batch(gshare_in.at[0:31], grad_r)
-    grad = jnp.sum(gshare_in[...], axis=0)
-    grad_ref[:, 0:384] = grad[0:4]
-    grad_ref[:, 384:768] = grad[4:8]
+    wait_batch(gpart.at[0], part_r)
+    for k in range(2):
+        grad_ref[:, k * 384:(k + 1) * 384] = jnp.where(parity == 0, gpart[k, 0:4], gpart[k, 4:8])
+    swap.wait_send()
 
 
 def fused(*args):
@@ -527,14 +532,16 @@
             pltpu.VMEM((32, 16, 768), bf16),
             pltpu.VMEM((4, 32, 256), bf16),
             pltpu.VMEM((8, 32, 256), bf16),
+            pltpu.VMEM((256, 256), bf16),
             pltpu.VMEM((8, 32, 896), bf16),
             pltpu.VMEM((8, 32, 896), bf16),
-            pltpu.VMEM((32, 768), bf16),
-            pltpu.VMEM((8, 32, 768), bf16),
+            pltpu.VMEM((2, 32, 384), bf16),
+            pltpu.VMEM((8, 32, 384), bf16),
             pltpu.VMEM((32, 8, 384), f32),
             pltpu.VMEM((32, 8, 384), f32),
+            pltpu.VMEM((2, 8, 384), f32),
             dma((17,)), dma((2, 2)), dma((2, 14)), dma((2, 2)), dma((2, 7)), dma((8,)), dma((4,)), dma((4,)),
-            *[dma] * 16,
+            *[dma] * 18,
         ],
         compiler_params=pltpu.CompilerParams(
             collective_id=0, has_side_effects=True, vmem_limit_bytes=52 * 1024 * 1024),

time: 96.4 us -> 94.6 us (0.981)
  Pallas kernels: 90 us -> 88.2 us
    pallas_call x1, Pallas kernels: 90 us -> 88.2 us  [fused(): pl.pallas_call(kernel, out_shape=(sds((1, 32), f32), sds((4, 768), f32),...]
where the time goes in v6:
time: 94.6 us; the launch traced here: 94.5 us
  Pallas kernels  88.2 us (93%)
  local copies, waits for them, and re-layouts  5.58 us (6%)
    pallas_call x1, Pallas kernels, fused(): pl.pallas_call(kernel, out_shape=(sds((1, 32), f32), sds((4, 768), f32),...  88.2 us
    unnamed x16, local copies, waits for them, and re-layouts  5.58 us

profile of v6, /device:TPU:1, one launch (start us, length us, event | category | flops | bytes accessed | tf_op | source)
XLA Modules:
  0.0 94.5 jit_solution(17138186867373165569)
XLA Ops:
  0.6 0.0 copy-start
  0.6 0.0 copy-start.1
  0.7 0.0 copy-start.2
  0.7 0.0 copy-start.3
  0.7 0.0 copy-start.4
  0.7 0.0 copy-start.5
  0.7 3.6 %copy.13 = bf16[128,8,2,512]{3,1,2,0:T(8,128)(2,1)} copy(bf16[128,8,2,512]{3,2,1,0:T(2,128)(2,1)} %bitcast.16) | data formatting | bytes 4194304
  4.3 0.0 copy-done
  4.3 0.0 copy-done.1
  4.3 0.0 copy-done.2
  4.3 0.0 copy-done.3
  4.3 0.0 copy-done.4
  4.3 0.0 copy-done.5
  4.3 88.2 %fused.1 = (f32[1,32]{1,0:T(1,128)S(1)}, f32[4,768]{1,0:T(4,128)S(1)}, bf16[32,16,768]{2,1,0:T(8,128)(2,1)S(1)}) custom-call(bf16[256,1024]{1,0:T(8,128)(2,1)S(1)} %copy-done, bf16[2048,1024]{1,0:T(8,128)(2,1)} %c_hbm.1, f32[1,1024]{1,0:T(1,128)S(1)} %bitcast.10, bf16[1024,1024]{1,0:T(8,128)(2,1)} %bitcast.17, bf16[512,1024]{1,0:T(8,128)(2,1)} %wout_hbm.1, ...), custom_call_target="tpu_custom_call" | custom-call | flops 11000000512 | bytes 20000000 | tf_op jit(solution)/shard_map/fused/pallas_call | solution.py:498
  92.5 0.5 copy.17
  93.1 0.9 copy.18
  93.9 0.6 copy.19
Async XLA Ops:
  0.6 3.6 %copy-start = (bf16[256,1024]{1,0:T(8,128)(2,1)S(1)}, bf16[256,1024]{1,0:T(8,128)(2,1)}, u32[]{:S(2)}) copy-start(bf16[256,1024]{1,0:T(8,128)(2,1)} %q_hbm.1) | copy-start | bytes 1572868
  0.6 3.6 %copy-start.1 = (f32[1024]{0:T(1024)S(1)}, f32[1024]{0:T(1024)}, u32[]{:S(2)}) copy-start(f32[1024]{0:T(1024)} %param.12) | copy-start | bytes 12292
  0.7 3.6 %copy-start.2 = (s32[32,8]{0,1:T(8,128)S(1)}, s32[32,8]{0,1:T(8,128)}, u32[]{:S(2)}) copy-start(s32[32,8]{0,1:T(8,128)} %param.17) | copy-start | bytes 3076
  0.7 3.6 %copy-start.3 = (s32[32,8]{0,1:T(8,128)S(1)}, s32[32,8]{0,1:T(8,128)}, u32[]{:S(2)}) copy-start(s32[32,8]{0,1:T(8,128)} %param.18) | copy-start | bytes 3076
  0.7 3.6 %copy-start.4 = (s32[256,1]{0,1:T(1,128)S(1)}, s32[256,1]{0,1:T(1,128)}, u32[]{:S(2)}) copy-start(s32[256,1]{0,1:T(1,128)} %param.19) | copy-start | bytes 3076
  0.7 3.6 %copy-start.5 = (s32[32]{0:T(128)S(1)}, s32[32]{0:T(128)}, u32[]{:S(2)}) copy-start(s32[32]{0:T(128)} %param.16) | copy-start | bytes 388

commit v7 on v6

--- a/solution.py
+++ b/solution.py
@@ -95,13 +95,12 @@
     def plane_copy(to, frm):
         return remote(codes.at[frm], codes.at[frm], plane_s, plane_r, {"dp": to})
 
-    def forward_q(k):
-        if k:
-            for h in (up(k), up(8 - k)):
-                wait_batch(qall.at[h], q_r.at[h])
-        for to, h, rows in ((right, up(8 - k) if k else z, pl.ds(0, 16)), (left, up(k), pl.ds(16, 16))):
-            block = qall.at[h] if k < 3 else qall.at[h, rows]
-            remote(block, block, q_s, q_r.at[h], {"mp": to}).start()
+    def send_q(h, to, rows=None):
+        block = qall.at[h] if rows is None else qall.at[h, rows]
+        remote(block, block, q_s, q_r.at[h], {"mp": to}).start()
+
+    def wait_q(h):
+        wait_batch(qall.at[h], q_r.at[h])
 
     def fetch_copy(pair, to, frm):
         return remote(fetch.at[pair, to], cands.at[pair, frm], fetch_s.at[pair], fetch_r.at[pair], {"dp": to})
@@ -225,8 +224,8 @@
         slot = lax.rem(i, 2)
         for n in range(2):
             rows = normed[slot]
-            gate = jnp.dot(rows, win[:, n * 256:(n + 1) * 256], preferred_element_type=f32)
-            upper = jnp.dot(rows, win[:, 512 + n * 256:768 + n * 256], preferred_element_type=f32)
+            gate = jnp.dot(rows, win[0, :, n * 256:(n + 1) * 256], preferred_element_type=f32)
+            upper = jnp.dot(rows, win[1, :, n * 256:(n + 1) * 256], preferred_element_type=f32)
             hidden[:, n * 256:(n + 1) * 256] = (gate / (1.0 + jnp.exp(-gate)) * upper).astype(bf16)
         normalise(jnp.minimum(i + 1, 8), 1 - slot)
 
@@ -326,7 +325,8 @@
     unit = raw / length
     embq[...] = unit.astype(bf16)
     qall[z] = embq[...]
-    forward_q(0)
+    for s in (2, 6, 1, 7):
+        send_q(z, up(s))
 
     for r in range(2):
         for way in (0, 1):
@@ -359,7 +359,6 @@
 
         cands[pair, d] = fetch[pair, d]
 
-    forward_q(1)
 
     turned = sumq[...].astype(f32).T.reshape(32, 4, 8, 32)
     for k in range(4):
@@ -371,7 +370,12 @@
 
     pieces_in[z] = pieces[z // 2]
     send_fetch(1)
-    forward_q(2)
+    wait_q(up(6))
+    send_q(up(6), up(1))
+    send_q(up(6), up(2), pl.ds(0, 16))
+    wait_q(up(2))
+    send_q(up(2), up(7))
+    send_q(up(2), up(6), pl.ds(16, 16))
 
     @pl.loop(0, 2)
     def _(s):
@@ -387,26 +391,12 @@
     pos_score = score_scale * jnp.sum(embq[...].astype(f32) * positive, axis=1, keepdims=True)
     pos_weight = jnp.exp(pos_score)
 
-    forward_q(3)
+    for s in (1, 7, 3, 5):
+        wait_q(up(s))
 
     @pl.loop(0, 4)
     def _(s):
         pair = pair_at(s)
-        wait_batch(cands.at[pair, 0:15], fetch_r.at[pair])
-        wait_batch(fetch.at[pair, 0:15], fetch_s.at[pair])
-
-        @pl.when(s < 2)
-        def _():
-            send_fetch(s + 2)
-
-        @pl.when(s == 1)
-        def _():
-            wait_batch(qall.at[up(4)], q_r.at[up(4)])
-
-        q = qall[pl.ds(pair * 2, 2)].reshape(64, 768)
-        cand = cands[pair].reshape(256, 768)
-        score = score_scale * lax.dot_general(
-            q, cand, (((1,), (1,)), ((), ())), preferred_element_type=f32)
         row = lax.broadcasted_iota(jnp.int32, (64, 256), 0)
         lane = lax.broadcasted_iota(jnp.int32, (64, 256), 1)
         slot = ((lane >> 4) * 8 + z) * 8 + (lane & 7)
@@ -415,6 +405,21 @@
         for k in range(1, 8):
             hit = hit | ((wants[:, k:k + 1] >> 8) == slot)
         hit = hit & ((row >> 5) == ((lane >> 3) & 1))
+        wait_batch(cands.at[pair, 0:15], fetch_r.at[pair])
+        wait_batch(fetch.at[pair, 0:15], fetch_s.at[pair])
+
+        @pl.when(s < 2)
+        def _():
+            send_fetch(s + 2)
+
+        @pl.when(s == 1)
+        def _():
+            wait_q(up(4))
+
+        q = qall[pl.ds(pair * 2, 2)].reshape(64, 768)
+        cand = cands[pair].reshape(256, 768)
+        score = score_scale * lax.dot_general(
+            q, cand, (((1,), (1,)), ((), ())), preferred_element_type=f32)
         weight = jnp.where(hit, jnp.exp(score), 0.0)
         total = jnp.sum(weight, axis=1, keepdims=True)
         summed = jnp.dot(weight.astype(bf16), cand, preferred_element_type=f32).astype(bf16)
@@ -502,7 +507,7 @@
         out_specs=[vmem, vmem, hbm],
         scratch_shapes=[
             pltpu.VMEM((9, 256, 1024), bf16),
-            pltpu.VMEM((1024, 1024), bf16),
+            pltpu.VMEM((2, 1024, 512), bf16),
             pltpu.VMEM((512, 1024), bf16),
             pltpu.VMEM((1024, 768), bf16),
             pltpu.VMEM((512, 768), bf16),
@@ -555,7 +560,7 @@
 ):
     width = queries.shape[1]
     loss, grad, index = fused(
-        queries, clips, norm_gain.reshape(1, width), w_in.reshape(width, -1), w_out, proj,
+        queries, clips, norm_gain.reshape(1, width), w_in.transpose(1, 0, 2), w_out, proj,
         pos_row.reshape(1, -1), neg_owner.T, neg_row.T, clip_dest.reshape(1, -1))
     return (loss.reshape(-1), index.reshape(-1, index.shape[-1]), grad)
 

time: 94.6 us -> 94.2 us (level)
  no operation moved by 1% of the time
where the time goes in v7:
time: 94.2 us; the launch traced here: 94.1 us
  Pallas kernels  88 us (93%)
  local copies, waits for them, and re-layouts  5.34 us (6%)
    pallas_call x1, Pallas kernels, fused(): pl.pallas_call(kernel, out_shape=(sds((1, 32), f32), sds((4, 768), f32),...  88 us
    unnamed x16, local copies, waits for them, and re-layouts  5.34 us

profile of v7, /device:TPU:1, one launch (start us, length us, event | category | flops | bytes accessed | tf_op | source)
XLA Modules:
  0.0 94.1 jit_solution(15858420396177907119)
XLA Ops:
  0.6 0.0 copy-start
  0.6 0.0 copy-start.1
  0.7 0.0 copy-start.2
  0.7 0.0 copy-start.3
  0.7 0.0 copy-start.4
  0.7 0.0 copy-start.5
  0.7 3.3 %copy.15 = bf16[1024,2,512]{2,0,1:T(8,128)(2,1)} copy(bf16[1024,2,512]{2,1,0:T(2,128)(2,1)} %param.13) | data formatting | bytes 4194304 | tf_op args[3]
  4.0 0.0 copy-done
  4.0 0.0 copy-done.1
  4.0 0.0 copy-done.2
  4.0 0.0 copy-done.3
  4.0 0.0 copy-done.4
  4.0 0.0 copy-done.5
  4.1 88.0 %fused.1 = (f32[1,32]{1,0:T(1,128)S(1)}, f32[4,768]{1,0:T(4,128)S(1)}, bf16[32,16,768]{2,1,0:T(8,128)(2,1)S(1)}) custom-call(bf16[256,1024]{1,0:T(8,128)(2,1)S(1)} %copy-done, bf16[2048,1024]{1,0:T(8,128)(2,1)} %c_hbm.1, f32[1,1024]{1,0:T(1,128)S(1)} %bitcast.11, bf16[2,1024,512]{2,1,0:T(8,128)(2,1)} %bitcast.17, bf16[512,1024]{1,0:T(8,128)(2,1)} %wout_hbm.1, ...), custom_call_target="tpu_custom_call" | custom-call | flops 11000000512 | bytes 20000000 | tf_op jit(solution)/shard_map/fused/pallas_call | solution.py:503
  92.1 0.5 copy.19
  92.6 0.9 copy.20
  93.5 0.6 copy.21
Async XLA Ops:
  0.6 3.4 %copy-start = (bf16[256,1024]{1,0:T(8,128)(2,1)S(1)}, bf16[256,1024]{1,0:T(8,128)(2,1)}, u32[]{:S(2)}) copy-start(bf16[256,1024]{1,0:T(8,128)(2,1)} %q_hbm.1) | copy-start | bytes 1572868
  0.6 3.4 %copy-start.1 = (f32[1024]{0:T(1024)S(1)}, f32[1024]{0:T(1024)}, u32[]{:S(2)}) copy-start(f32[1024]{0:T(1024)} %param.12) | copy-start | bytes 12292
  0.7 3.4 %copy-start.2 = (s32[32,8]{0,1:T(8,128)S(1)}, s32[32,8]{0,1:T(8,128)}, u32[]{:S(2)}) copy-start(s32[32,8]{0,1:T(8,128)} %param.17) | copy-start | bytes 3076
  0.7 3.4 %copy-start.3 = (s32[32,8]{0,1:T(8,128)S(1)}, s32[32,8]{0,1:T(8,128)}, u32[]{:S(2)}) copy-start(s32[32,8]{0,1:T(8,128)} %param.18) | copy-start | bytes 3076
  0.7 3.4 %copy-start.4 = (s32[256,1]{0,1:T(1,128)S(1)}, s32[256,1]{0,1:T(1,128)}, u32[]{:S(2)}) copy-start(s32[256,1]{0,1:T(1,128)} %param.19) | copy-start | bytes 3076
  0.7 3.4 %copy-start.5 = (s32[32]{0:T(128)S(1)}, s32[32]{0:T(128)}, u32[]{:S(2)}) copy-start(s32[32]{0:T(128)} %param.16) | copy-start | bytes 388
